TPU v7x, 128 devices: a whole 4x4x4 slice. The times are simulated.
128 devices in a mesh: gx: 8 (over z, core), gy: 16 (over x, y).
Axes of the slice: x: 4, y: 4, z: 4, core: 2. Of those that a mesh axis runs over, the one named last changes fastest.
Arguments:
- pressure_previous: float32 [128, 512, 128], P('gx', 'gy'), may hold values from -6 to 6
- pressure_current: float32 [128, 512, 128], P('gx', 'gy'), may hold values from -6 to 6
- adjoint_next: float32 [128, 512, 128], P('gx', 'gy'), may hold values from -6 to 6
- adjoint_current: float32 [128, 512, 128], P('gx', 'gy'), may hold values from -6 to 6
- inverse_modulus: float32 [128, 512, 128], P('gx', 'gy'), may hold values from 0.5 to 2
- inverse_density: float32 [128, 512, 128], P('gx', 'gy'), may hold values from 0.5 to 2
- face_mask: int32 [6, 16, 64, 16], P(None, 'gx', 'gy'), may hold values 0 or 1
Outputs:
- density_kernel: float32 [128, 512, 128], P('gx', 'gy')
- modulus_kernel: float32 [128, 512, 128], P('gx', 'gy')
- impedance_kernel: float32 [128, 512, 128], P('gx', 'gy')
All inputs are finite; a program needn't handle non-finite values. No bound on the sum of `face_mask` on one device may be relied on, other than what follows from the above.
Results may differ from a plain program's by a relative error of at most 0.0001.
Values sent between devices are 32-bit elements; how exact they have to be, the bound alone decides.
A program may use at most 128 MiB of HBM per device.

v0:
```python
import functools

import jax
import jax.numpy as jnp
import numpy as np
from jax import lax
from jax.experimental import pallas as pl
from jax.experimental.pallas import tpu as pltpu
from jax.sharding import PartitionSpec as P

MESH = pl.DeviceIdType.MESH
F32 = jnp.float32
BF16 = jnp.bfloat16
NODES = 8
STEPS = 8
LANES = 128
CHUNK = 2

TIME_STEP = 0.01
GLL_POINTS = (
    -1.0,
    -0.8717401485096066,
    -0.5917001814331423,
    -0.2092992179024789,
    0.2092992179024789,
    0.5917001814331423,
    0.8717401485096066,
    1.0,
)
GLL_WEIGHTS = (
    0.03571428571428571,
    0.2107042271435061,
    0.3411226924835044,
    0.4124587946587038,
    0.4124587946587038,
    0.3411226924835044,
    0.2107042271435061,
    0.03571428571428571,
)


def gll_derivative():
    points = np.array(GLL_POINTS)
    previous_poly = np.ones(NODES)
    current_poly = points.copy()
    for degree in range(1, NODES - 1):
        next_poly = ((2 * degree + 1) * points * current_poly - degree * previous_poly) / (
            degree + 1
        )
        previous_poly, current_poly = (current_poly, next_poly)
    matrix = np.zeros((NODES, NODES))
    for row_index in range(NODES):
        for col_index in range(NODES):
            if row_index != col_index:
                matrix[row_index, col_index] = current_poly[row_index] / (
                    current_poly[col_index] * (points[row_index] - points[col_index])
                )
    matrix[0, 0] = -NODES * (NODES - 1) / 4.0
    matrix[NODES - 1, NODES - 1] = NODES * (NODES - 1) / 4.0
    return matrix


DERIVATIVE = gll_derivative()


def halves(matrix):
    near, far = matrix[:4, :4], matrix[:4, 7:3:-1]
    return (near - far) / 2, (near + far) / 2


FORWARD = halves(DERIVATIVE)
BACKWARD = halves(DERIVATIVE.T)


def apply_eight(values, blocks):
    odd, even = blocks
    sums = [values[j] + values[7 - j] for j in range(4)]
    diffs = [values[j] - values[7 - j] for j in range(4)]
    low, high = [], []
    for i in range(4):
        a = diffs[0] * float(odd[i, 0])
        b = sums[0] * float(even[i, 0])
        for j in range(1, 4):
            a = a + diffs[j] * float(odd[i, j])
            b = b + sums[j] * float(even[i, j])
        low.append(a + b)
        high.append(a - b)
    return low + high[::-1]


def third_tables():
    count = LANES // NODES
    block = np.kron(np.eye(count), DERIVATIVE)
    assembly = np.eye(LANES)
    for k in range(1, count):
        assembly[8 * k, 8 * k - 1] = 1.0
        assembly[8 * k - 1, 8 * k] = 1.0
    tables = []
    for table in (block.T, block @ assembly):
        high = table.astype(BF16)
        low = (table - high.astype(np.float64)).astype(BF16)
        both = np.concatenate([high, low], axis=1)
        tables.append(np.concatenate([both, both], axis=0))
    return np.stack(tables)


def roll_sub(values, shift):
    shift %= 8
    return values if shift == 0 else pltpu.roll(values, shift, values.ndim - 2)


def kernel(
    shape_xy,
    up_ref,
    uc_ref,
    an_ref,
    ac_ref,
    im_ref,
    id_ref,
    fm_ref,
    tab_ref,
    dens_ref,
    mod_ref,
    imp_ref,
    nat,
    mask,
    table,
    cx,
    cy,
    cz,
    scale,
    keep,
    kx,
    ky,
    uf,
    vf,
    aa,
    va,
    gu,
    ga,
    acc,
    fx,
    fy,
    sp_x,
    sp_y,
    kn_x,
    kn_y,
    sums,
    xs0,
    ys0,
    ds0,
    xr0,
    yr0,
    dr0,
    xrk,
    yrk,
    xs,
    ys,
    ds,
    xr,
    yr,
    dr,
    in_sem,
    out_sem,
    send0,
    recv0,
    sendk,
    recvk,
    send,
    recv,
):
    count_x, count_y = shape_xy
    gx, gy = lax.axis_index("gx"), lax.axis_index("gy")

    in_x = {0: gx > 0, 1: gx < count_x - 1}
    in_y = {0: gy > 0, 1: gy < count_y - 1}
    other_x = gx + 1 - 2 * lax.rem(gx, 2)
    other_y = gy + 1 - 2 * lax.rem(gy, 2)

    def target_x(side):
        here = in_x[side]
        step = 2 * side - 1
        device = (jnp.where(here, gx + step, gx), jnp.where(here, gy, other_y))
        return device, jnp.where(here, 1 - side, side)

    def target_y(side):
        here = in_y[side]
        step = 2 * side - 1
        device = (jnp.where(here, gx, other_x), jnp.where(here, gy + step, gy))
        return device, jnp.where(here, 1 - side, side)

    def target_d(side_x, side_y):
        hx, hy = in_x[side_x], in_y[side_y]
        both_out = jnp.logical_not(jnp.logical_or(hx, hy))
        dx = jnp.where(both_out, count_x - 1 - gx, jnp.where(hx, gx + 2 * side_x - 1, gx))
        dy = jnp.where(hy, gy + 2 * side_y - 1, gy)
        slot_x = jnp.where(jnp.logical_or(hx, both_out), 1 - side_x, side_x)
        slot_y = jnp.where(hy, 1 - side_y, side_y)
        return (dx, dy), slot_x * 2 + slot_y

    targets_x = [target_x(0), target_x(1)]
    targets_y = [target_y(0), target_y(1)]
    targets_d = [target_d(0, 0), target_d(0, 1), target_d(1, 0), target_d(1, 1)]

    loads = []
    for k, ref in enumerate((id_ref, im_ref, uc_ref, up_ref, ac_ref, an_ref)):
        for half in range(2):
            loads.append(
                pltpu.make_async_copy(
                    ref.at[pl.ds(8 * half, 8)],
                    nat.at[k, :, pl.ds(32 * half, 32), :],
                    in_sem.at[2 * k + half],
                )
            )
    loads.append(pltpu.make_async_copy(fm_ref, mask, in_sem.at[12]))
    loads.append(pltpu.make_async_copy(tab_ref, table, in_sem.at[13]))
    for load in loads:
        load.start()
    barrier = pltpu.get_barrier_semaphore()
    for device, _ in targets_x + targets_y + targets_d:
        pl.semaphore_signal(barrier, inc=1, device_id=device, device_id_type=MESH)

    sub = lax.broadcasted_iota(jnp.int32, (8, LANES), 0)
    lane = lax.broadcasted_iota(jnp.int32, (8, LANES), 1)
    ey = sub % 4
    low_x = sub < 4
    zplace = lane % 8
    z_low = jnp.logical_and(zplace == 0, lane > 0)
    z_high = jnp.logical_and(zplace == 7, lane < LANES - 1)
    zero = jnp.zeros((8, LANES), F32)
    wz = zero
    for j in range(NODES):
        wz = jnp.where(zplace == j, F32(GLL_WEIGHTS[j]), wz)

    def one_if(flag):
        return jnp.where(flag, 1, 0)

    halo_x = [sub < 4 * one_if(in_x[0]), sub >= 8 - 4 * one_if(in_x[1])]
    halo_y = [ey < one_if(in_y[0]), ey >= 4 - one_if(in_y[1])]
    halo_d = [
        jnp.logical_and(halo_x[0], halo_y[0]),
        jnp.logical_and(halo_x[0], halo_y[1]),
        jnp.logical_and(halo_x[1], halo_y[0]),
        jnp.logical_and(halo_x[1], halo_y[1]),
    ]
    node_d = ((0, 0, 0, 1), (0, 7, 3, -1), (7, 0, 4, 1), (7, 7, 7, -1))

    def sum_third(values):
        before = pltpu.roll(values, 1, values.ndim - 1)
        after = pltpu.roll(values, LANES - 1, values.ndim - 1)
        return values + jnp.where(z_low, before, jnp.where(z_high, after, 0.0))

    def join_x(first, last):
        return (
            first + jnp.where(low_x, 0.0, roll_sub(last, 4)),
            last + jnp.where(low_x, roll_sub(first, 4), 0.0),
        )

    def join_y(first, last):
        return (
            first + jnp.where(ey == 0, 0.0, roll_sub(last, 1)),
            last + jnp.where(ey == 3, 0.0, roll_sub(first, 7)),
        )

    def pack_x(first, last):
        return (
            jnp.where(low_x, first[0:4], roll_sub(first[4:8], 4)),
            jnp.where(low_x, roll_sub(last[0:4], 4), last[4:8]),
        )

    def unpack_x(side, packed):
        turned = roll_sub(packed, 4)
        pair = [packed, turned] if side == 0 else [turned, packed]
        return jnp.concatenate(pair, axis=0)

    def pack_y(first, last):
        first = first.reshape(2, 4, 8, LANES)
        last = last.reshape(2, 4, 8, LANES)
        low, high = first[:, 0], roll_sub(last[:, 0], 5)
        for j in range(1, 4):
            low = jnp.where(ey == j, roll_sub(first[:, j], j), low)
            high = jnp.where(ey == j, roll_sub(last[:, j], 5 + j), high)
        return low, high

    def unpack_y(side, packed):
        rows = [roll_sub(packed, 3 * side - j) for j in range(4)]
        return jnp.stack(rows, axis=1).reshape(8, 8, LANES)

    def corner_lines(n00, n07, n70, n77):
        return jnp.where(low_x, jnp.where(ey == 0, n00, n07), jnp.where(ey == 0, n70, n77))

    def messages(src, dst, ssem, rsem):
        out = []
        for side in range(2):
            device, slot = targets_x[side]
            out.append((src[0].at[side], dst[0].at[slot], side, slot, device))
        for side in range(2):
            device, slot = targets_y[side]
            out.append((src[1].at[side], dst[1].at[slot], 2 + side, 2 + slot, device))
        if src[2] is not None:
            for k in range(4):
                device, slot = targets_d[k]
                out.append((src[2], dst[2].at[slot], 4 + k, 4 + slot, device))
        return [
            pltpu.make_async_remote_copy(
                src_ref=a,
                dst_ref=b,
                send_sem=ssem.at[i],
                recv_sem=rsem.at[j],
                device_id=device,
                device_id_type=MESH,
            )
            for a, b, i, j, device in out
        ]

    def arrive(src, dst, ssem, rsem):
        pairs = [(src[0].at[side], dst[0].at[side], side) for side in range(2)]
        pairs += [(src[1].at[side], dst[1].at[side], 2 + side) for side in range(2)]
        if src[2] is not None:
            pairs += [(src[2], dst[2].at[k], 4 + k) for k in range(4)]
        for a, b, i in pairs:
            copy = pltpu.make_async_remote_copy(
                src_ref=a,
                dst_ref=b,
                send_sem=ssem.at[i],
                recv_sem=rsem.at[i],
                device_id=targets_x[0][0],
                device_id_type=MESH,
            )
            copy.wait_recv()
            copy.wait_send()

    homes = (cz, scale, keep, uf, vf.at[1], aa.at[8], va)

    def natural(k, ix, iy):
        return nat[k, ix, pl.ds(iy, 8, stride=8), :]

    half_x = [jnp.where(jnp.logical_or(halo_x[0], jnp.logical_not(low_x)), 0.5, 1.0), 1.0]
    half_x_high = jnp.where(jnp.logical_or(halo_x[1], low_x), 0.5, 1.0)
    half_y_low = jnp.where(jnp.logical_or(halo_y[0], ey != 0), 0.5, 1.0)
    half_y_high = jnp.where(jnp.logical_or(halo_y[1], ey != 3), 0.5, 1.0)
    half_z = jnp.where(jnp.logical_or(z_low, z_high), 0.5, 1.0)

    def share(ix, iy):
        value = half_z
        if ix == 0:
            value = value * half_x[0]
        if ix == 7:
            value = value * half_x_high
        if iy == 0:
            value = value * half_y_low
        if iy == 7:
            value = value * half_y_high
        return value

    for load in loads[0:2]:
        load.wait()
    for ix in range(8):
        for iy in range(8):
            raw = natural(0, ix, iy) * (wz * float(GLL_WEIGHTS[ix] * GLL_WEIGHTS[iy]))
            summed = sum_third(raw)
            cz[ix, iy] = raw
            cx[ix, iy] = summed
            cy[ix, iy] = summed
    for load in loads[2:4]:
        load.wait()
    for ix in range(8):
        for iy in range(8):
            raw = natural(1, ix, iy) * (wz * float(GLL_WEIGHTS[ix] * GLL_WEIGHTS[iy]))
            scale[ix, iy] = sum_third(raw)
    loads[12].wait()
    loads[13].wait()
    spread = jnp.where(
        lax.broadcasted_iota(jnp.int32, (16, LANES), 1) // 8
        == lax.broadcasted_iota(jnp.int32, (16, LANES), 0),
        1.0,
        0.0,
    ).astype(F32)
    faces = []
    for f in range(6):
        cells = jnp.concatenate([mask[f, 0], mask[f, 1]], axis=0).astype(F32)
        faces.append(jnp.dot(cells, spread, preferred_element_type=F32))
    third_face = sum_third(jnp.where(zplace == 0, faces[4], jnp.where(zplace == 7, faces[5], 0.0)))
    faces = [sum_third(wz * face) for face in faces[:4]]
    for ix in range(8):
        for iy in range(8):
            value = third_face * float(GLL_WEIGHTS[ix] * GLL_WEIGHTS[iy])
            if ix == 0:
                value = value + faces[0] * float(GLL_WEIGHTS[iy])
            if ix == 7:
                value = value + faces[1] * float(GLL_WEIGHTS[iy])
            if iy == 0:
                value = value + faces[2] * float(GLL_WEIGHTS[ix])
            if iy == 7:
                value = value + faces[3] * float(GLL_WEIGHTS[ix])
            keep[ix, iy] = value
    for k in range(2, 6):
        for load in loads[2 * k : 2 * k + 2]:
            load.wait()
        home = homes[k + 1]
        for ix in range(8):
            for iy in range(8):
                home[ix, iy] = sum_third(natural(k, ix, iy) * share(ix, iy))

    def join_first(home):
        first, last = join_x(home[0], home[7])
        home[0] = first
        home[7] = last

    def join_second(home):
        first, last = join_y(home[:, 0], home[:, 7])
        home[:, 0] = first
        home[:, 7] = last

    for f, home in enumerate(homes):
        join_first(home)
        join_second(home)
        xs0[0, f], xs0[1, f] = pack_x(home[0], home[7])
        ys0[0, f], ys0[1, f] = pack_y(home[:, 0], home[:, 7])
        ds0[f] = corner_lines(home[0, 0], home[0, 7], home[7, 0], home[7, 7])
    join_first(cy)
    xs0[0, 7], xs0[1, 7] = pack_x(cy[0], cy[7])
    join_second(cx)
    ys0[0, 7], ys0[1, 7] = pack_y(cx[:, 0], cx[:, 7])

    pl.semaphore_wait(barrier, 8)
    for copy in messages((xs0, ys0, ds0), (xr0, yr0, dr0), send0, recv0):
        copy.start()
    arrive((xs0, ys0, ds0), (xr0, yr0, dr0), send0, recv0)

    def add_x(home, f):
        home[0] = home[0] + jnp.where(halo_x[0], unpack_x(0, xr0[0, f]), 0.0)
        home[7] = home[7] + jnp.where(halo_x[1], unpack_x(1, xr0[1, f]), 0.0)

    def add_y(home, f):
        home[:, 0] = home[:, 0] + jnp.where(halo_y[0], unpack_y(0, yr0[0, f]), 0.0)
        home[:, 7] = home[:, 7] + jnp.where(halo_y[1], unpack_y(1, yr0[1, f]), 0.0)

    for f, home in enumerate(homes):
        add_x(home, f)
        add_y(home, f)
        for k, (ix, iy, _, turn) in enumerate(node_d):
            home[ix, iy] = home[ix, iy] + jnp.where(halo_d[k], roll_sub(dr0[k, f], turn), 0.0)
    add_x(cy, 7)
    add_y(cx, 7)

    for ix in range(8):
        mass = scale[ix]
        one_over = 1.0 / mass
        scale[ix] = (TIME_STEP * TIME_STEP) * one_over
        keep[ix] = 1.0 - TIME_STEP * keep[ix] * one_over
        vf[1, ix] = uf[ix] - vf[1, ix]
        va[ix] = aa[8, ix] - va[ix]

    end_x = [
        jnp.where(low_x, F32(DERIVATIVE[i, 0]), F32(DERIVATIVE[i, 7])) for i in range(8)
    ]
    end_y = [
        jnp.where(ey < 2, F32(DERIVATIVE[i, 0]), F32(DERIVATIVE[i, 7])) for i in range(8)
    ]
    for c in range(0, 8, CHUNK):
        here = slice(c, c + CHUNK)
        rows = apply_eight([end_x[i] * cx[i, here] for i in range(8)], BACKWARD)
        for j in range(8):
            kx[j, here] = rows[j]
        rows = apply_eight([end_y[i] * cy[here, i] for i in range(8)], BACKWARD)
        for j in range(8):
            ky[here, j] = rows[j]
    fx[0], fx[1] = kx[0], kx[7]
    fy[0], fy[1] = ky[:, 0], ky[:, 7]

    def put_faces(side_x, side_y, fx0, fx1, fy0, fy1):
        side_x[0], side_x[1] = pack_x(fx0, fx1)
        side_y[0], side_y[1] = pack_y(fy0, fy1)

    xsk, ysk = xs0.at[:, 0], ys0.at[:, 0]
    put_faces(xsk, ysk, fx[0], fx[1], fy[0], fy[1])
    for copy in messages((xsk, ysk, None), (xrk, yrk, None), sendk, recvk):
        copy.start()

    def third(source, gradient):
        def times(values, which):
            high = values.astype(BF16)
            low = (values - high.astype(F32)).astype(BF16)
            both = jnp.dot(
                jnp.concatenate([high, low], axis=1), table[which], preferred_element_type=F32
            )
            return both[:, :LANES] + both[:, LANES:]

        slope = times(source[...].reshape(512, LANES), 0)
        gradient[2] = slope.reshape(8, 8, 8, LANES)
        if acc is not None:
            flux = cz[...].reshape(512, LANES) * slope
            acc[...] = times(flux, 1).reshape(8, 8, 8, LANES)

    def first_part(source, gradient, halos):
        for c in range(0, 8, CHUNK):
            here = slice(c, c + CHUNK)
            slopes = apply_eight([source[j, here] for j in range(8)], FORWARD)
            for j in range(8):
                gradient[0, j, here] = slopes[j]
            image = apply_eight([cx[j, here] * slopes[j] for j in range(8)], BACKWARD)
            if halos is None:
                fx[0, here], fx[1, here] = image[0], image[7]
            image[0], image[7] = join_x(image[0], image[7])
            if halos is not None:
                image[0] = image[0] + halos[0][here]
                image[7] = image[7] + halos[1][here]
            for j in range(8):
                acc[j, here] = acc[j, here] + image[j]

    def second_part(source, gradient, halos, v_from, u_to, v_to):
        for c in range(0, 8, CHUNK):
            here = slice(c, c + CHUNK)
            now = [source[here, j] for j in range(8)]
            slopes = apply_eight(now, FORWARD)
            for j in range(8):
                gradient[1, here, j] = slopes[j]
            image = apply_eight([cy[here, j] * slopes[j] for j in range(8)], BACKWARD)
            if halos is None:
                fy[0, here], fy[1, here] = image[0], image[7]
            image[0], image[7] = join_y(image[0], image[7])
            if halos is not None:
                image[0] = image[0] + halos[0][here]
                image[7] = image[7] + halos[1][here]
            for j in range(8):
                change = keep[here, j] * v_from[here, j] - scale[here, j] * (acc[here, j] + image[j])
                v_to[here, j] = change
                u_to[here, j] = now[j] + change

    def begin(field, turn, source, gradient, v_from, u_to, v_to):
        slot = lax.rem(turn, 2)
        third(source, gradient)
        first_part(source, gradient, None)
        second_part(source, gradient, None, v_from, u_to, v_to)
        own_x = [fx[0], fx[1]]
        own_y = [fy[0], fy[1]]
        to_x, to_y, to_d = xs.at[field, slot], ys.at[field, slot], ds.at[field, slot]
        put_faces(to_x.at[:, 0], to_y.at[:, 0], own_x[0], own_x[1], own_y[0], own_y[1])
        next_x = kx[0] * u_to[0]
        next_y = ky[:, 0] * u_to[:, 0]
        for j in range(1, 8):
            next_x = next_x + kx[j] * u_to[j]
            next_y = next_y + ky[:, j] * u_to[:, j]
        put_faces(to_x.at[:, 1], to_y.at[:, 1], next_x, next_x, next_y, next_y)
        for side, node in ((0, 0), (1, 7)):
            sp_x[field, side] = scale[node] * own_x[side]
            sp_y[field, side] = scale[:, node] * own_y[side]
        along_x = [jnp.sum(kx[:, n] * sp_y[field, s], axis=0) for s, n in ((0, 0), (1, 7))]
        along_y = [jnp.sum(ky[n] * sp_x[field, s], axis=0) for s, n in ((0, 0), (1, 7))]
        to_d[...] = -(
            jnp.where(ey == 0, along_x[0], along_x[1]) + jnp.where(low_x, along_y[0], along_y[1])
        )
        for copy in messages(
            (to_x, to_y, to_d),
            (xr.at[field, slot], yr.at[field, slot], dr.at[field, slot]),
            send.at[field, slot],
            recv.at[field, slot],
        ):
            copy.start()

    def complete(field, turn, u, v):
        slot = lax.rem(turn, 2)
        from_x, from_y, from_d = xr.at[field, slot], yr.at[field, slot], dr.at[field, slot]
        arrive(
            (xs.at[field, slot], ys.at[field, slot], ds.at[field, slot]),
            (from_x, from_y, from_d),
            send.at[field, slot],
            recv.at[field, slot],
        )
        for side, node in ((0, 0), (1, 7)):
            part = scale[node] * jnp.where(halo_x[side], unpack_x(side, from_x[side, 0]), 0.0)
            u[node] = u[node] - part
            v[node] = v[node] - part
        for side, node in ((0, 0), (1, 7)):
            part = scale[:, node] * jnp.where(halo_y[side], unpack_y(side, from_y[side, 0]), 0.0)
            u[:, node] = u[:, node] - part
            v[:, node] = v[:, node] - part
        return from_x, from_y, from_d

    def finish(field, arrived, source, gradient, v_from, u_to, v_to):
        from_x, from_y, from_d = arrived
        third(source, gradient)
        halos_x, halos_y = [], []
        for side in range(2):
            part = unpack_x(side, from_x[side, 1]) - kn_x[side] * sp_x[field, side]
            halos_x.append(jnp.where(halo_x[side], part, 0.0))
            part = unpack_y(side, from_y[side, 1]) - kn_y[side] * sp_y[field, side]
            halos_y.append(jnp.where(halo_y[side], part, 0.0))
        first_part(source, gradient, halos_x)
        for k, (ix, iy, _, turn) in enumerate(node_d):
            acc[ix, iy] = acc[ix, iy] + jnp.where(halo_d[k], roll_sub(from_d[k], turn), 0.0)
        second_part(source, gradient, halos_y, v_from, u_to, v_to)

    def begin_u(turn):
        n = 2 * turn + 1
        begin(0, turn, uf, gu.at[n], vf.at[n], uf, vf.at[n + 1])

    def begin_a(turn):
        n = 8 - 2 * turn
        begin(1, turn, aa.at[n], ga.at[n], va, aa.at[n - 1], va)

    def finish_u(turn):
        n = 2 * turn + 2
        arrived = complete(0, turn, uf, vf.at[n])
        finish(0, arrived, uf, gu.at[n], vf.at[n], uf, vf.at[n + 1])

    def finish_a(turn):
        n = 7 - 2 * turn
        arrived = complete(1, turn, aa.at[n], va)
        finish(1, arrived, aa.at[n], ga.at[n], va, aa.at[n - 1], va)

    begin_u(0)
    begin_a(0)
    arrive((xsk, ysk, None), (xrk, yrk, None), sendk, recvk)
    for side in range(2):
        kn_x[side] = unpack_x(side, xrk[side])
        kn_y[side] = unpack_y(side, yrk[side])

    def cycle(turn, carry):
        finish_u(turn)
        begin_u(turn + 1)
        finish_a(turn)
        begin_a(turn + 1)
        return carry

    lax.fori_loop(0, STEPS // 2 - 1, cycle, 0)

    def density_of(ns, ix):
        total = None
        for n in ns:
            for d in range(3):
                term = gu[n, d, ix] * ga[n, d, ix]
                total = term if total is None else total + term
        return total

    def moduli_of(ns, ix):
        modulus, impedance = None, None
        for n in ns:
            now, before, after = aa[n, ix], vf[n, ix], vf[n + 1, ix]
            a, b = now * (after - before), now * (after + before)
            modulus = a if modulus is None else modulus + a
            impedance = b if impedance is None else impedance + b
        return modulus, impedance

    for ix in range(8):
        sums[0, ix] = density_of(range(2, 8), ix)
        sums[1, ix], sums[2, ix] = moduli_of(range(2, 7), ix)

    last = STEPS // 2 - 1
    finish_u(last)
    complete(1, last, aa.at[1], va)
    source, gradient = aa.at[1], ga.at[1]
    high = source[...].reshape(512, LANES).astype(BF16)
    low = (source[...].reshape(512, LANES) - high.astype(F32)).astype(BF16)
    both = jnp.dot(jnp.concatenate([high, low], axis=1), table[0], preferred_element_type=F32)
    gradient[2] = (both[:, :LANES] + both[:, LANES:]).reshape(8, 8, 8, LANES)
    for c in range(0, 8, CHUNK):
        here = slice(c, c + CHUNK)
        slopes = apply_eight([source[j, here] for j in range(8)], FORWARD)
        for j in range(8):
            gradient[0, j, here] = slopes[j]
        slopes = apply_eight([source[here, j] for j in range(8)], FORWARD)
        for j in range(8):
            gradient[1, here, j] = slopes[j]

    for ix in range(8):
        density = sums[0, ix] + density_of((1, 8), ix)
        modulus, impedance = moduli_of((1, 7, 8), ix)
        modulus = sums[1, ix] + modulus
        impedance = (sums[2, ix] + impedance) * (1.0 - keep[ix])
        for iy in range(8):
            weight = wz * float(TIME_STEP * GLL_WEIGHTS[ix] * GLL_WEIGHTS[iy])
            rows = pl.ds(iy, 8, stride=8)
            nat[0, ix, rows, :] = weight * density[iy]
            nat[1, ix, rows, :] = modulus[iy]
            nat[2, ix, rows, :] = impedance[iy]
    stores = []
    for k, ref in enumerate((dens_ref, mod_ref, imp_ref)):
        for half in range(2):
            stores.append(
                pltpu.make_async_copy(
                    nat.at[k, :, pl.ds(32 * half, 32), :],
                    ref.at[pl.ds(8 * half, 8)],
                    out_sem.at[2 * k + half],
                )
            )
    for store in stores:
        store.start()
    for store in stores:
        store.wait()


def field(*lead):
    return pltpu.VMEM((*lead, 8, 8, 8, LANES), F32)


def per_device(shape_xy, *args):
    local = args[0].shape
    out = jax.ShapeDtypeStruct(local, F32)
    tables = jnp.asarray(third_tables())
    any_spec = pl.BlockSpec(memory_space=pl.ANY)
    vectors = lambda *lead: pltpu.VMEM((*lead, 8, LANES), F32)
    return pl.pallas_call(
        functools.partial(kernel, shape_xy),
        out_shape=(out, out, out),
        in_specs=[any_spec] * 8,
        out_specs=(any_spec,) * 3,
        scratch_shapes=[
            pltpu.VMEM((6, 8, 64, LANES), F32),
            pltpu.VMEM(args[6].shape, jnp.int32),
            pltpu.VMEM(tables.shape, BF16),
            field(),
            field(),
            field(),
            field(),
            field(),
            field(),
            field(),
            field(),
            field(10),
            field(9),
            field(),
            field(9, 3),
            field(9, 3),
            field(),
            vectors(2, 8),
            vectors(2, 8),
            vectors(2, 2, 8),
            vectors(2, 2, 8),
            vectors(2, 8),
            vectors(2, 8),
            field(3),
            vectors(2, 8, 4),
            vectors(2, 8, 2),
            vectors(7),
            vectors(2, 8, 4),
            vectors(2, 8, 2),
            vectors(4, 7),
            vectors(2, 4),
            vectors(2, 2),
            vectors(2, 2, 2, 2, 4),
            vectors(2, 2, 2, 2, 2),
            vectors(2, 2),
            vectors(2, 2, 2, 2, 4),
            vectors(2, 2, 2, 2, 2),
            vectors(2, 2, 4),
            pltpu.SemaphoreType.DMA((14,)),
            pltpu.SemaphoreType.DMA((6,)),
            pltpu.SemaphoreType.DMA((8,)),
            pltpu.SemaphoreType.DMA((8,)),
            pltpu.SemaphoreType.DMA((4,)),
            pltpu.SemaphoreType.DMA((4,)),
            pltpu.SemaphoreType.DMA((2, 2, 8)),
            pltpu.SemaphoreType.DMA((2, 2, 8)),
        ],
        compiler_params=pltpu.CompilerParams(
            collective_id=0, has_side_effects=True, vmem_limit_bytes=48 * 1024 * 1024
        ),
    )(*args, tables)


def solution(mesh):
    shape_xy = (mesh.shape["gx"], mesh.shape["gy"])
    in_specs = (P("gx", "gy", None),) * 6 + (P(None, "gx", "gy", None),)
    out_specs = (P("gx", "gy", None),) * 3
    return jax.shard_map(
        functools.partial(per_device, shape_xy),
        mesh=mesh,
        in_specs=in_specs,
        out_specs=out_specs,
        check_vma=False,
    )
```

profile of v0, /device:TPU:7, one launch (start us, length us, event | category | flops | bytes accessed | tf_op | source)
XLA Modules:
  0.0 44.9 jit_solution(1301166451787176182)
XLA Ops:
  0.6 0.0 copy-start
  0.6 0.9 %copy-done = f32[16,32,128]{2,1,0:T(8,128)S(1)} copy-done((f32[16,32,128]{2,1,0:T(8,128)S(1)}, f32[16,32,128]{2,1,0:T(8,128)}, u32[]{:S(2)}) %copy-start) | copy-done | bytes 262168
  1.6 0.0 copy-start.1
  1.6 0.9 %copy-done.1 = f32[16,32,128]{2,1,0:T(8,128)S(1)} copy-done((f32[16,32,128]{2,1,0:T(8,128)S(1)}, f32[16,32,128]{2,1,0:T(8,128)}, u32[]{:S(2)}) %copy-start.1) | copy-done | bytes 262168
  2.5 0.0 copy-start.2
  2.5 0.9 %copy-done.2 = f32[16,32,128]{2,1,0:T(8,128)S(1)} copy-done((f32[16,32,128]{2,1,0:T(8,128)S(1)}, f32[16,32,128]{2,1,0:T(8,128)}, u32[]{:S(2)}) %copy-start.2) | copy-done | bytes 262168
  3.5 0.0 copy-start.3
  3.5 0.9 %copy-done.3 = f32[16,32,128]{2,1,0:T(8,128)S(1)} copy-done((f32[16,32,128]{2,1,0:T(8,128)S(1)}, f32[16,32,128]{2,1,0:T(8,128)}, u32[]{:S(2)}) %copy-start.3) | copy-done | bytes 262168
  4.4 0.0 copy-start.4
  4.4 0.9 %copy-done.4 = f32[16,32,128]{2,1,0:T(8,128)S(1)} copy-done((f32[16,32,128]{2,1,0:T(8,128)S(1)}, f32[16,32,128]{2,1,0:T(8,128)}, u32[]{:S(2)}) %copy-start.4) | copy-done | bytes 262168
  5.4 0.0 copy-start.5
  5.4 0.9 %copy-done.5 = f32[16,32,128]{2,1,0:T(8,128)S(1)} copy-done((f32[16,32,128]{2,1,0:T(8,128)S(1)}, f32[16,32,128]{2,1,0:T(8,128)}, u32[]{:S(2)}) %copy-start.5) | copy-done | bytes 262168
  6.3 0.0 copy-start.6
  6.3 0.9 %copy-done.6 = bf16[2,256,256]{2,1,0:T(8,128)(2,1)S(1)} copy-done((bf16[2,256,256]{2,1,0:T(8,128)(2,1)S(1)}, bf16[2,256,256]{2,1,0:T(8,128)(2,1)}, u32[]{:S(2)}) %copy-start.6) | copy-done | bytes 262168
  7.3 0.0 copy-start.7
  7.3 0.7 %copy-done.7 = s32[6,2,4,16]{3,2,1,0:T(4,128)S(1)} copy-done((s32[6,2,4,16]{3,2,1,0:T(4,128)S(1)}, s32[6,2,4,16]{3,2,1,0:T(4,128)}, u32[]{:S(2)}) %copy-start.7) | copy-done | bytes 3096
  8.0 34.7 %shard_map.103 = (f32[16,32,128]{2,1,0:T(8,128)S(1)}, f32[16,32,128]{2,1,0:T(8,128)S(1)}, f32[16,32,128]{2,1,0:T(8,128)S(1)}) custom-call(f32[16,32,128]{2,1,0:T(8,128)S(1)} %copy-done, f32[16,32,128]{2,1,0:T(8,128)S(1)} %copy-done.1, f32[16,32,128]{2,1,0:T(8,128)S(1)} %copy-done.2, f32[16,32,128]{2,1,0:T(8,128)S(1)} %copy-done.3, ...), custom_call_target="tpu_custom_call" | custom-call | tf_op jit(solution)/shard_map/pallas_call | solution.py:704
  42.8 0.7 %copy.14 = f32[16,32,128]{2,1,0:T(8,128)} copy(f32[16,32,128]{2,1,0:T(8,128)S(1)} %get-tuple-element.6) | data formatting | bytes 524288
  43.5 0.7 %copy.15 = f32[16,32,128]{2,1,0:T(8,128)} copy(f32[16,32,128]{2,1,0:T(8,128)S(1)} %get-tuple-element.7) | data formatting | bytes 524288
  44.2 0.7 %copy.16 = f32[16,32,128]{2,1,0:T(8,128)} copy(f32[16,32,128]{2,1,0:T(8,128)S(1)} %get-tuple-element.8) | data formatting | bytes 524288
Async XLA Ops:
  0.6 1.0 %copy-start = (f32[16,32,128]{2,1,0:T(8,128)S(1)}, f32[16,32,128]{2,1,0:T(8,128)}, u32[]{:S(2)}) copy-start(f32[16,32,128]{2,1,0:T(8,128)} %up_ref.1) | copy-start | bytes 786436
  1.6 0.9 %copy-start.1 = (f32[16,32,128]{2,1,0:T(8,128)S(1)}, f32[16,32,128]{2,1,0:T(8,128)}, u32[]{:S(2)}) copy-start(f32[16,32,128]{2,1,0:T(8,128)} %uc_ref.1) | copy-start | bytes 786436
  2.5 0.9 %copy-start.2 = (f32[16,32,128]{2,1,0:T(8,128)S(1)}, f32[16,32,128]{2,1,0:T(8,128)}, u32[]{:S(2)}) copy-start(f32[16,32,128]{2,1,0:T(8,128)} %an_ref.1) | copy-start | bytes 786436
  3.5 0.9 %copy-start.3 = (f32[16,32,128]{2,1,0:T(8,128)S(1)}, f32[16,32,128]{2,1,0:T(8,128)}, u32[]{:S(2)}) copy-start(f32[16,32,128]{2,1,0:T(8,128)} %ac_ref.1) | copy-start | bytes 786436
  4.4 0.9 %copy-start.4 = (f32[16,32,128]{2,1,0:T(8,128)S(1)}, f32[16,32,128]{2,1,0:T(8,128)}, u32[]{:S(2)}) copy-start(f32[16,32,128]{2,1,0:T(8,128)} %im_ref.1) | copy-start | bytes 786436
  5.4 0.9 %copy-start.5 = (f32[16,32,128]{2,1,0:T(8,128)S(1)}, f32[16,32,128]{2,1,0:T(8,128)}, u32[]{:S(2)}) copy-start(f32[16,32,128]{2,1,0:T(8,128)} %id_ref.1) | copy-start | bytes 786436
  6.3 0.9 %copy-start.6 = (bf16[2,256,256]{2,1,0:T(8,128)(2,1)S(1)}, bf16[2,256,256]{2,1,0:T(8,128)(2,1)}, u32[]{:S(2)}) copy-start(bf16[2,256,256]{2,1,0:T(8,128)(2,1)} %constant.2.clone.tab_ref) | copy-start | bytes 786436
  7.3 0.7 %copy-start.7 = (s32[6,2,4,16]{3,2,1,0:T(4,128)S(1)}, s32[6,2,4,16]{3,2,1,0:T(4,128)}, u32[]{:S(2)}) copy-start(s32[6,2,4,16]{3,2,1,0:T(4,128)} %fm_ref.1) | copy-start | bytes 9220
where the time goes:
time: 45.3 us; the launch traced here: 44.9 us
  Pallas kernels  34.7 us (77%)
  local copies, waits for them, and re-layouts  9.49 us (21%)
  between operations  0.66 us (1%)
    pallas_call x1, Pallas kernels, per_device(): pl.pallas_call(functools.partial(kernel, shape_xy), out_shape=(out, out,...  34.7 us
    unnamed x19, local copies, waits for them, and re-layouts  9.49 us

commit v1 on v0

--- a/solution.py
+++ b/solution.py
@@ -88,22 +88,6 @@
     return low + high[::-1]
 
 
-def third_tables():
-    count = LANES // NODES
-    block = np.kron(np.eye(count), DERIVATIVE)
-    assembly = np.eye(LANES)
-    for k in range(1, count):
-        assembly[8 * k, 8 * k - 1] = 1.0
-        assembly[8 * k - 1, 8 * k] = 1.0
-    tables = []
-    for table in (block.T, block @ assembly):
-        high = table.astype(BF16)
-        low = (table - high.astype(np.float64)).astype(BF16)
-        both = np.concatenate([high, low], axis=1)
-        tables.append(np.concatenate([both, both], axis=0))
-    return np.stack(tables)
-
-
 def roll_sub(values, shift):
     shift %= 8
     return values if shift == 0 else pltpu.roll(values, shift, values.ndim - 2)
@@ -118,7 +102,6 @@
     im_ref,
     id_ref,
     fm_ref,
-    tab_ref,
     dens_ref,
     mod_ref,
     imp_ref,
@@ -139,8 +122,6 @@
     gu,
     ga,
     acc,
-    fx,
-    fy,
     sp_x,
     sp_y,
     kn_x,
@@ -149,9 +130,13 @@
     xs0,
     ys0,
     ds0,
+    xs1,
+    ys1,
     xr0,
     yr0,
     dr0,
+    xr1,
+    yr1,
     xrk,
     yrk,
     xs,
@@ -161,7 +146,6 @@
     yr,
     dr,
     in_sem,
-    out_sem,
     send0,
     recv0,
     sendk,
@@ -213,7 +197,6 @@
                 )
             )
     loads.append(pltpu.make_async_copy(fm_ref, mask, in_sem.at[12]))
-    loads.append(pltpu.make_async_copy(tab_ref, table, in_sem.at[13]))
     for load in loads:
         load.start()
     barrier = pltpu.get_barrier_semaphore()
@@ -232,6 +215,29 @@
     for j in range(NODES):
         wz = jnp.where(zplace == j, F32(GLL_WEIGHTS[j]), wz)
 
+    def sum_third(values):
+        before = pltpu.roll(values, 1, values.ndim - 1)
+        after = pltpu.roll(values, LANES - 1, values.ndim - 1)
+        return values + jnp.where(z_low, before, jnp.where(z_high, after, 0.0))
+
+    tiles = [zero, zero]
+    for i in range(8):
+        for j in range(8):
+            value = F32(DERIVATIVE[i, j])
+            tiles[0] = jnp.where(jnp.logical_and(sub == j, zplace == i), value, tiles[0])
+            tiles[1] = jnp.where(jnp.logical_and(sub == i, zplace == j), value, tiles[1])
+    for which in range(2):
+        rows = [jnp.where(lane // 8 == k, tiles[which], 0.0) for k in range(LANES // 8)]
+        if which == 1:
+            rows = [sum_third(row) for row in rows]
+        block = jnp.concatenate(rows, axis=0)
+        high = block.astype(BF16)
+        low = (block - high.astype(F32)).astype(BF16)
+        for half in range(2):
+            here = slice(LANES * half, LANES * half + LANES)
+            table[which, here, :LANES] = high
+            table[which, here, LANES:] = low
+
     def one_if(flag):
         return jnp.where(flag, 1, 0)
 
@@ -245,11 +251,6 @@
     ]
     node_d = ((0, 0, 0, 1), (0, 7, 3, -1), (7, 0, 4, 1), (7, 7, 7, -1))
 
-    def sum_third(values):
-        before = pltpu.roll(values, 1, values.ndim - 1)
-        after = pltpu.roll(values, LANES - 1, values.ndim - 1)
-        return values + jnp.where(z_low, before, jnp.where(z_high, after, 0.0))
-
     def join_x(first, last):
         return (
             first + jnp.where(low_x, 0.0, roll_sub(last, 4)),
@@ -289,7 +290,7 @@
     def corner_lines(n00, n07, n70, n77):
         return jnp.where(low_x, jnp.where(ey == 0, n00, n07), jnp.where(ey == 0, n70, n77))
 
-    def messages(src, dst, ssem, rsem):
+    def copies(src, dst, ssem, rsem, first):
         out = []
         for side in range(2):
             device, slot = targets_x[side]
@@ -297,40 +298,40 @@
         for side in range(2):
             device, slot = targets_y[side]
             out.append((src[1].at[side], dst[1].at[slot], 2 + side, 2 + slot, device))
-        if src[2] is not None:
+        if len(src) > 2:
             for k in range(4):
                 device, slot = targets_d[k]
                 out.append((src[2], dst[2].at[slot], 4 + k, 4 + slot, device))
-        return [
+        for a, b, i, j, device in out:
             pltpu.make_async_remote_copy(
                 src_ref=a,
                 dst_ref=b,
-                send_sem=ssem.at[i],
-                recv_sem=rsem.at[j],
+                send_sem=ssem.at[first + i],
+                recv_sem=rsem.at[first + j],
                 device_id=device,
                 device_id_type=MESH,
-            )
-            for a, b, i, j, device in out
-        ]
-
-    def arrive(src, dst, ssem, rsem):
-        pairs = [(src[0].at[side], dst[0].at[side], side) for side in range(2)]
-        pairs += [(src[1].at[side], dst[1].at[side], 2 + side) for side in range(2)]
-        if src[2] is not None:
-            pairs += [(src[2], dst[2].at[k], 4 + k) for k in range(4)]
-        for a, b, i in pairs:
-            copy = pltpu.make_async_remote_copy(
-                src_ref=a,
-                dst_ref=b,
-                send_sem=ssem.at[i],
-                recv_sem=rsem.at[i],
-                device_id=targets_x[0][0],
-                device_id_type=MESH,
-            )
-            copy.wait_recv()
-            copy.wait_send()
+            ).start()
+
+    def arrive(src, dst, ssem, rsem, first, which=range(8)):
+        pairs = [(src[0].at[side], dst[0].at[side]) for side in range(2)]
+        pairs += [(src[1].at[side], dst[1].at[side]) for side in range(2)]
+        if len(src) > 2:
+            pairs += [(src[2], dst[2].at[k]) for k in range(4)]
+        for i, (a, b) in enumerate(pairs):
+            if i in which:
+                copy = pltpu.make_async_remote_copy(
+                    src_ref=a,
+                    dst_ref=b,
+                    send_sem=ssem.at[first + i],
+                    recv_sem=rsem.at[first + i],
+                    device_id=targets_x[0][0],
+                    device_id_type=MESH,
+                )
+                copy.wait_recv()
+                copy.wait_send()
 
     homes = (cz, scale, keep, uf, vf.at[1], aa.at[8], va)
+    groups = ((0, 1, 2), (3, 4), (5, 6))
 
     def natural(k, ix, iy):
         return nat[k, ix, pl.ds(iy, 8, stride=8), :]
@@ -369,7 +370,6 @@
             raw = natural(1, ix, iy) * (wz * float(GLL_WEIGHTS[ix] * GLL_WEIGHTS[iy]))
             scale[ix, iy] = sum_third(raw)
     loads[12].wait()
-    loads[13].wait()
     spread = jnp.where(
         lax.broadcasted_iota(jnp.int32, (16, LANES), 1) // 8
         == lax.broadcasted_iota(jnp.int32, (16, LANES), 0),
@@ -394,14 +394,6 @@
             if iy == 7:
                 value = value + faces[3] * float(GLL_WEIGHTS[ix])
             keep[ix, iy] = value
-    for k in range(2, 6):
-        for load in loads[2 * k : 2 * k + 2]:
-            load.wait()
-        home = homes[k + 1]
-        for ix in range(8):
-            for iy in range(8):
-                home[ix, iy] = sum_third(natural(k, ix, iy) * share(ix, iy))
-
     def join_first(home):
         first, last = join_x(home[0], home[7])
         home[0] = first
@@ -412,45 +404,62 @@
         home[:, 0] = first
         home[:, 7] = last
 
-    for f, home in enumerate(homes):
+    def pack_field(f):
+        home = homes[f]
         join_first(home)
         join_second(home)
         xs0[0, f], xs0[1, f] = pack_x(home[0], home[7])
         ys0[0, f], ys0[1, f] = pack_y(home[:, 0], home[:, 7])
         ds0[f] = corner_lines(home[0, 0], home[0, 7], home[7, 0], home[7, 7])
+
+    def group_refs(g):
+        here = pl.ds(groups[g][0], len(groups[g]))
+        src = (xs0.at[:, here], ys0.at[:, here], ds0.at[here])
+        dst = (xr0.at[:, here], yr0.at[:, here], dr0.at[:, here])
+        return src, dst, send0, recv0, 8 * g
+
+    for f in groups[0]:
+        pack_field(f)
     join_first(cy)
-    xs0[0, 7], xs0[1, 7] = pack_x(cy[0], cy[7])
     join_second(cx)
-    ys0[0, 7], ys0[1, 7] = pack_y(cx[:, 0], cx[:, 7])
-
+    one_sided = ((xs1, ys1), (xr1, yr1), send0, recv0, 24)
+    xs1[0], xs1[1] = pack_x(cy[0], cy[7])
+    ys1[0], ys1[1] = pack_y(cx[:, 0], cx[:, 7])
     pl.semaphore_wait(barrier, 8)
-    for copy in messages((xs0, ys0, ds0), (xr0, yr0, dr0), send0, recv0):
-        copy.start()
-    arrive((xs0, ys0, ds0), (xr0, yr0, dr0), send0, recv0)
-
-    def add_x(home, f):
-        home[0] = home[0] + jnp.where(halo_x[0], unpack_x(0, xr0[0, f]), 0.0)
-        home[7] = home[7] + jnp.where(halo_x[1], unpack_x(1, xr0[1, f]), 0.0)
-
-    def add_y(home, f):
-        home[:, 0] = home[:, 0] + jnp.where(halo_y[0], unpack_y(0, yr0[0, f]), 0.0)
-        home[:, 7] = home[:, 7] + jnp.where(halo_y[1], unpack_y(1, yr0[1, f]), 0.0)
-
-    for f, home in enumerate(homes):
-        add_x(home, f)
-        add_y(home, f)
+    copies(*one_sided)
+    copies(*group_refs(0))
+
+    for g in (1, 2):
+        for f in groups[g]:
+            k = f - 1
+            for load in loads[2 * k : 2 * k + 2]:
+                load.wait()
+            home = homes[f]
+            for ix in range(8):
+                for iy in range(8):
+                    home[ix, iy] = sum_third(natural(k, ix, iy) * share(ix, iy))
+            pack_field(f)
+        copies(*group_refs(g))
+
+    def add_x(home, received):
+        for side, node in ((0, 0), (1, 7)):
+            home[node] = home[node] + jnp.where(halo_x[side], unpack_x(side, received[side]), 0.0)
+
+    def add_y(home, received):
+        for side, node in ((0, 0), (1, 7)):
+            part = jnp.where(halo_y[side], unpack_y(side, received[side]), 0.0)
+            home[:, node] = home[:, node] + part
+
+    def add_field(f):
+        home = homes[f]
+        add_x(home, xr0.at[:, f])
+        add_y(home, yr0.at[:, f])
         for k, (ix, iy, _, turn) in enumerate(node_d):
             home[ix, iy] = home[ix, iy] + jnp.where(halo_d[k], roll_sub(dr0[k, f], turn), 0.0)
-    add_x(cy, 7)
-    add_y(cx, 7)
-
-    for ix in range(8):
-        mass = scale[ix]
-        one_over = 1.0 / mass
-        scale[ix] = (TIME_STEP * TIME_STEP) * one_over
-        keep[ix] = 1.0 - TIME_STEP * keep[ix] * one_over
-        vf[1, ix] = uf[ix] - vf[1, ix]
-        va[ix] = aa[8, ix] - va[ix]
+
+    arrive(*one_sided)
+    add_x(cy, xr1)
+    add_y(cx, yr1)
 
     end_x = [
         jnp.where(low_x, F32(DERIVATIVE[i, 0]), F32(DERIVATIVE[i, 7])) for i in range(8)
@@ -466,50 +475,47 @@
         rows = apply_eight([end_y[i] * cy[here, i] for i in range(8)], BACKWARD)
         for j in range(8):
             ky[here, j] = rows[j]
-    fx[0], fx[1] = kx[0], kx[7]
-    fy[0], fy[1] = ky[:, 0], ky[:, 7]
-
     def put_faces(side_x, side_y, fx0, fx1, fy0, fy1):
         side_x[0], side_x[1] = pack_x(fx0, fx1)
         side_y[0], side_y[1] = pack_y(fy0, fy1)
 
-    xsk, ysk = xs0.at[:, 0], ys0.at[:, 0]
-    put_faces(xsk, ysk, fx[0], fx[1], fy[0], fy[1])
-    for copy in messages((xsk, ysk, None), (xrk, yrk, None), sendk, recvk):
-        copy.start()
-
-    def third(source, gradient):
-        def times(values, which):
-            high = values.astype(BF16)
-            low = (values - high.astype(F32)).astype(BF16)
-            both = jnp.dot(
-                jnp.concatenate([high, low], axis=1), table[which], preferred_element_type=F32
-            )
-            return both[:, :LANES] + both[:, LANES:]
-
+    ends = ((xs1, ys1), (xrk, yrk), sendk, recvk, 0)
+    put_faces(xs1, ys1, kx[0], kx[7], ky[:, 0], ky[:, 7])
+    copies(*ends)
+    arrive(*group_refs(0))
+    for f in groups[0]:
+        add_field(f)
+    for ix in range(8):
+        one_over = 1.0 / scale[ix]
+        scale[ix] = (TIME_STEP * TIME_STEP) * one_over
+        keep[ix] = 1.0 - TIME_STEP * keep[ix] * one_over
+    arrive(*group_refs(1))
+    for f in groups[1]:
+        add_field(f)
+    for ix in range(8):
+        vf[1, ix] = uf[ix] - vf[1, ix]
+
+    def times(values, which):
+        high = values.astype(BF16)
+        low = (values - high.astype(F32)).astype(BF16)
+        both = jnp.dot(
+            jnp.concatenate([high, low], axis=1), table[which], preferred_element_type=F32
+        )
+        return both[:, :LANES] + both[:, LANES:]
+
+    def advance(source, gradient, v_from, u_to, v_to):
         slope = times(source[...].reshape(512, LANES), 0)
         gradient[2] = slope.reshape(8, 8, 8, LANES)
-        if acc is not None:
-            flux = cz[...].reshape(512, LANES) * slope
-            acc[...] = times(flux, 1).reshape(8, 8, 8, LANES)
-
-    def first_part(source, gradient, halos):
+        acc[...] = times(cz[...].reshape(512, LANES) * slope, 1).reshape(8, 8, 8, LANES)
         for c in range(0, 8, CHUNK):
             here = slice(c, c + CHUNK)
             slopes = apply_eight([source[j, here] for j in range(8)], FORWARD)
             for j in range(8):
                 gradient[0, j, here] = slopes[j]
             image = apply_eight([cx[j, here] * slopes[j] for j in range(8)], BACKWARD)
-            if halos is None:
-                fx[0, here], fx[1, here] = image[0], image[7]
             image[0], image[7] = join_x(image[0], image[7])
-            if halos is not None:
-                image[0] = image[0] + halos[0][here]
-                image[7] = image[7] + halos[1][here]
             for j in range(8):
                 acc[j, here] = acc[j, here] + image[j]
-
-    def second_part(source, gradient, halos, v_from, u_to, v_to):
         for c in range(0, 8, CHUNK):
             here = slice(c, c + CHUNK)
             now = [source[here, j] for j in range(8)]
@@ -517,80 +523,87 @@
             for j in range(8):
                 gradient[1, here, j] = slopes[j]
             image = apply_eight([cy[here, j] * slopes[j] for j in range(8)], BACKWARD)
-            if halos is None:
-                fy[0, here], fy[1, here] = image[0], image[7]
             image[0], image[7] = join_y(image[0], image[7])
-            if halos is not None:
-                image[0] = image[0] + halos[0][here]
-                image[7] = image[7] + halos[1][here]
             for j in range(8):
                 change = keep[here, j] * v_from[here, j] - scale[here, j] * (acc[here, j] + image[j])
                 v_to[here, j] = change
                 u_to[here, j] = now[j] + change
 
+    def face_rows(u):
+        along_x, along_y = kx[0] * u[0], ky[:, 0] * u[:, 0]
+        for j in range(1, 8):
+            along_x = along_x + kx[j] * u[j]
+            along_y = along_y + ky[:, j] * u[:, j]
+        return along_x, along_y
+
+    def mail(kind, field, slot):
+        src = [xs.at[kind, field, slot], ys.at[kind, field, slot]]
+        dst = [xr.at[kind, field, slot], yr.at[kind, field, slot]]
+        if kind == 0:
+            src.append(ds.at[field, slot])
+            dst.append(dr.at[field, slot])
+        return src, dst, send.at[field, slot], recv.at[field, slot], 8 * kind
+
     def begin(field, turn, source, gradient, v_from, u_to, v_to):
         slot = lax.rem(turn, 2)
-        third(source, gradient)
-        first_part(source, gradient, None)
-        second_part(source, gradient, None, v_from, u_to, v_to)
-        own_x = [fx[0], fx[1]]
-        own_y = [fy[0], fy[1]]
-        to_x, to_y, to_d = xs.at[field, slot], ys.at[field, slot], ds.at[field, slot]
-        put_faces(to_x.at[:, 0], to_y.at[:, 0], own_x[0], own_x[1], own_y[0], own_y[1])
-        next_x = kx[0] * u_to[0]
-        next_y = ky[:, 0] * u_to[:, 0]
-        for j in range(1, 8):
-            next_x = next_x + kx[j] * u_to[j]
-            next_y = next_y + ky[:, j] * u_to[:, j]
-        put_faces(to_x.at[:, 1], to_y.at[:, 1], next_x, next_x, next_y, next_y)
+        first, second = mail(0, field, slot), mail(1, field, slot)
+        own_x, own_y = face_rows(source)
+        put_faces(first[0][0], first[0][1], own_x, own_x, own_y, own_y)
         for side, node in ((0, 0), (1, 7)):
-            sp_x[field, side] = scale[node] * own_x[side]
-            sp_y[field, side] = scale[:, node] * own_y[side]
-        along_x = [jnp.sum(kx[:, n] * sp_y[field, s], axis=0) for s, n in ((0, 0), (1, 7))]
-        along_y = [jnp.sum(ky[n] * sp_x[field, s], axis=0) for s, n in ((0, 0), (1, 7))]
-        to_d[...] = -(
-            jnp.where(ey == 0, along_x[0], along_x[1]) + jnp.where(low_x, along_y[0], along_y[1])
+            sp_x[field, side] = scale[node] * own_x
+            sp_y[field, side] = scale[:, node] * own_y
+        lines_x = [jnp.sum(kx[:, n] * sp_y[field, s], axis=0) for s, n in ((0, 0), (1, 7))]
+        lines_y = [jnp.sum(ky[n] * sp_x[field, s], axis=0) for s, n in ((0, 0), (1, 7))]
+        ds[field, slot] = -(
+            jnp.where(ey == 0, lines_x[0], lines_x[1]) + jnp.where(low_x, lines_y[0], lines_y[1])
         )
-        for copy in messages(
-            (to_x, to_y, to_d),
-            (xr.at[field, slot], yr.at[field, slot], dr.at[field, slot]),
-            send.at[field, slot],
-            recv.at[field, slot],
-        ):
-            copy.start()
-
-    def complete(field, turn, u, v):
-        slot = lax.rem(turn, 2)
-        from_x, from_y, from_d = xr.at[field, slot], yr.at[field, slot], dr.at[field, slot]
-        arrive(
-            (xs.at[field, slot], ys.at[field, slot], ds.at[field, slot]),
-            (from_x, from_y, from_d),
-            send.at[field, slot],
-            recv.at[field, slot],
-        )
-        for side, node in ((0, 0), (1, 7)):
-            part = scale[node] * jnp.where(halo_x[side], unpack_x(side, from_x[side, 0]), 0.0)
+        copies(*first)
+        advance(source, gradient, v_from, u_to, v_to)
+        next_x, next_y = face_rows(u_to)
+        put_faces(second[0][0], second[0][1], next_x, next_x, next_y, next_y)
+        copies(*second)
+
+    def mend(u, v, parts_x, parts_y):
+        for node, part in zip((0, 7), parts_x):
+            part = scale[node] * part
             u[node] = u[node] - part
             v[node] = v[node] - part
-        for side, node in ((0, 0), (1, 7)):
-            part = scale[:, node] * jnp.where(halo_y[side], unpack_y(side, from_y[side, 0]), 0.0)
+        for node, part in zip((0, 7), parts_y):
+            part = scale[:, node] * part
             u[:, node] = u[:, node] - part
             v[:, node] = v[:, node] - part
-        return from_x, from_y, from_d
-
-    def finish(field, arrived, source, gradient, v_from, u_to, v_to):
-        from_x, from_y, from_d = arrived
-        third(source, gradient)
-        halos_x, halos_y = [], []
-        for side in range(2):
-            part = unpack_x(side, from_x[side, 1]) - kn_x[side] * sp_x[field, side]
-            halos_x.append(jnp.where(halo_x[side], part, 0.0))
-            part = unpack_y(side, from_y[side, 1]) - kn_y[side] * sp_y[field, side]
-            halos_y.append(jnp.where(halo_y[side], part, 0.0))
-        first_part(source, gradient, halos_x)
-        for k, (ix, iy, _, turn) in enumerate(node_d):
-            acc[ix, iy] = acc[ix, iy] + jnp.where(halo_d[k], roll_sub(from_d[k], turn), 0.0)
-        second_part(source, gradient, halos_y, v_from, u_to, v_to)
+
+    def complete(field, turn, u, v):
+        letter = mail(0, field, lax.rem(turn, 2))
+        arrive(*letter, range(4))
+        from_x, from_y = letter[1][:2]
+        mend(
+            u,
+            v,
+            [jnp.where(halo_x[s], unpack_x(s, from_x[s]), 0.0) for s in range(2)],
+            [jnp.where(halo_y[s], unpack_y(s, from_y[s]), 0.0) for s in range(2)],
+        )
+
+    def finish(field, turn, source, gradient, v_from, u_to, v_to):
+        slot = lax.rem(turn, 2)
+        advance(source, gradient, v_from, u_to, v_to)
+        first, second = mail(0, field, slot), mail(1, field, slot)
+        arrive(*second)
+        from_x, from_y = second[1]
+        parts_x, parts_y = [], []
+        for s in range(2):
+            part = unpack_x(s, from_x[s]) - kn_x[s] * sp_x[field, s]
+            parts_x.append(jnp.where(halo_x[s], part, 0.0))
+            part = unpack_y(s, from_y[s]) - kn_y[s] * sp_y[field, s]
+            parts_y.append(jnp.where(halo_y[s], part, 0.0))
+        mend(u_to, v_to, parts_x, parts_y)
+        arrive(*first, range(4, 8))
+        from_d = first[1][2]
+        for k, (ix, iy, _, turn_by) in enumerate(node_d):
+            line = jnp.where(halo_d[k], roll_sub(from_d[k], turn_by), 0.0)
+            part = scale[ix, iy] * line
+            u_to[ix, iy] = u_to[ix, iy] - part
+            v_to[ix, iy] = v_to[ix, iy] - part
 
     def begin_u(turn):
         n = 2 * turn + 1
@@ -602,17 +615,22 @@
 
     def finish_u(turn):
         n = 2 * turn + 2
-        arrived = complete(0, turn, uf, vf.at[n])
-        finish(0, arrived, uf, gu.at[n], vf.at[n], uf, vf.at[n + 1])
+        complete(0, turn, uf, vf.at[n])
+        finish(0, turn, uf, gu.at[n], vf.at[n], uf, vf.at[n + 1])
 
     def finish_a(turn):
         n = 7 - 2 * turn
-        arrived = complete(1, turn, aa.at[n], va)
-        finish(1, arrived, aa.at[n], ga.at[n], va, aa.at[n - 1], va)
+        complete(1, turn, aa.at[n], va)
+        finish(1, turn, aa.at[n], ga.at[n], va, aa.at[n - 1], va)
 
     begin_u(0)
+    arrive(*group_refs(2))
+    for f in groups[2]:
+        add_field(f)
+    for ix in range(8):
+        va[ix] = aa[8, ix] - va[ix]
     begin_a(0)
-    arrive((xsk, ysk, None), (xrk, yrk, None), sendk, recvk)
+    arrive(*ends)
     for side in range(2):
         kn_x[side] = unpack_x(side, xrk[side])
         kn_y[side] = unpack_y(side, yrk[side])
@@ -650,11 +668,10 @@
     last = STEPS // 2 - 1
     finish_u(last)
     complete(1, last, aa.at[1], va)
+    arrive(*mail(0, 1, last % 2), range(4, 8))
+    arrive(*mail(1, 1, last % 2))
     source, gradient = aa.at[1], ga.at[1]
-    high = source[...].reshape(512, LANES).astype(BF16)
-    low = (source[...].reshape(512, LANES) - high.astype(F32)).astype(BF16)
-    both = jnp.dot(jnp.concatenate([high, low], axis=1), table[0], preferred_element_type=F32)
-    gradient[2] = (both[:, :LANES] + both[:, LANES:]).reshape(8, 8, 8, LANES)
+    gradient[2] = times(source[...].reshape(512, LANES), 0).reshape(8, 8, 8, LANES)
     for c in range(0, 8, CHUNK):
         here = slice(c, c + CHUNK)
         slopes = apply_eight([source[j, here] for j in range(8)], FORWARD)
@@ -672,19 +689,22 @@
         for iy in range(8):
             weight = wz * float(TIME_STEP * GLL_WEIGHTS[ix] * GLL_WEIGHTS[iy])
             rows = pl.ds(iy, 8, stride=8)
-            nat[0, ix, rows, :] = weight * density[iy]
-            nat[1, ix, rows, :] = modulus[iy]
-            nat[2, ix, rows, :] = impedance[iy]
-    stores = []
-    for k, ref in enumerate((dens_ref, mod_ref, imp_ref)):
-        for half in range(2):
-            stores.append(
-                pltpu.make_async_copy(
-                    nat.at[k, :, pl.ds(32 * half, 32), :],
-                    ref.at[pl.ds(8 * half, 8)],
-                    out_sem.at[2 * k + half],
-                )
-            )
+            dens_ref[ix, rows, :] = weight * density[iy]
+            mod_ref[ix, rows, :] = modulus[iy]
+            imp_ref[ix, rows, :] = impedance[iy]
+
+
+def deliver(*refs):
+    parts, outs, sem = refs[:3], refs[3:6], refs[6]
+    stores = [
+        pltpu.make_async_copy(
+            parts[k].at[:, pl.ds(32 * half, 32), :],
+            outs[k].at[pl.ds(8 * half, 8)],
+            sem.at[2 * k + half],
+        )
+        for k in range(3)
+        for half in range(2)
+    ]
     for store in stores:
         store.start()
     for store in stores:
@@ -696,20 +716,19 @@
 
 
 def per_device(shape_xy, *args):
-    local = args[0].shape
-    out = jax.ShapeDtypeStruct(local, F32)
-    tables = jnp.asarray(third_tables())
-    any_spec = pl.BlockSpec(memory_space=pl.ANY)
     vectors = lambda *lead: pltpu.VMEM((*lead, 8, LANES), F32)
-    return pl.pallas_call(
+    hbm = pl.BlockSpec(memory_space=pltpu.HBM)
+    vmem = pl.BlockSpec(memory_space=pltpu.VMEM)
+    operands = [pltpu.with_memory_space_constraint(a, pltpu.HBM) for a in args]
+    parts = pl.pallas_call(
         functools.partial(kernel, shape_xy),
-        out_shape=(out, out, out),
-        in_specs=[any_spec] * 8,
-        out_specs=(any_spec,) * 3,
+        out_shape=(pltpu.VMEM((8, 64, LANES), F32),) * 3,
+        in_specs=[hbm] * 7,
+        out_specs=(vmem,) * 3,
         scratch_shapes=[
             pltpu.VMEM((6, 8, 64, LANES), F32),
             pltpu.VMEM(args[6].shape, jnp.int32),
-            pltpu.VMEM(tables.shape, BF16),
+            pltpu.VMEM((2, 2 * LANES, 2 * LANES), BF16),
             field(),
             field(),
             field(),
@@ -724,19 +743,21 @@
             field(9, 3),
             field(9, 3),
             field(),
-            vectors(2, 8),
-            vectors(2, 8),
             vectors(2, 2, 8),
             vectors(2, 2, 8),
             vectors(2, 8),
             vectors(2, 8),
             field(3),
-            vectors(2, 8, 4),
-            vectors(2, 8, 2),
+            vectors(2, 7, 4),
+            vectors(2, 7, 2),
             vectors(7),
-            vectors(2, 8, 4),
-            vectors(2, 8, 2),
+            vectors(2, 4),
+            vectors(2, 2),
+            vectors(2, 7, 4),
+            vectors(2, 7, 2),
             vectors(4, 7),
+            vectors(2, 4),
+            vectors(2, 2),
             vectors(2, 4),
             vectors(2, 2),
             vectors(2, 2, 2, 2, 4),
@@ -745,19 +766,25 @@
             vectors(2, 2, 2, 2, 4),
             vectors(2, 2, 2, 2, 2),
             vectors(2, 2, 4),
-            pltpu.SemaphoreType.DMA((14,)),
-            pltpu.SemaphoreType.DMA((6,)),
-            pltpu.SemaphoreType.DMA((8,)),
-            pltpu.SemaphoreType.DMA((8,)),
+            pltpu.SemaphoreType.DMA((13,)),
+            pltpu.SemaphoreType.DMA((28,)),
+            pltpu.SemaphoreType.DMA((28,)),
             pltpu.SemaphoreType.DMA((4,)),
             pltpu.SemaphoreType.DMA((4,)),
-            pltpu.SemaphoreType.DMA((2, 2, 8)),
-            pltpu.SemaphoreType.DMA((2, 2, 8)),
+            pltpu.SemaphoreType.DMA((2, 2, 12)),
+            pltpu.SemaphoreType.DMA((2, 2, 12)),
         ],
         compiler_params=pltpu.CompilerParams(
             collective_id=0, has_side_effects=True, vmem_limit_bytes=48 * 1024 * 1024
         ),
-    )(*args, tables)
+    )(*operands)
+    return pl.pallas_call(
+        deliver,
+        out_shape=(pltpu.HBM(args[0].shape, F32),) * 3,
+        in_specs=[pl.BlockSpec(memory_space=pl.ANY)] * 3,
+        out_specs=(hbm,) * 3,
+        scratch_shapes=[pltpu.SemaphoreType.DMA((6,))],
+    )(*[pltpu.with_memory_space_constraint(part, pltpu.VMEM) for part in parts])
 
 
 def solution(mesh):

time: 45.3 us -> 32.9 us (0.73)
  local copies, waits for them, and re-layouts: 9.49 us -> 0 us
  Pallas kernels: 34.7 us -> 32.1 us
    unnamed x19 -> x0, local copies, waits for them, and re-layouts: 9.49 us -> none
    pallas_call x1 -> x2, Pallas kernels: 34.7 us -> 32.1 us  [the longest x1 31.2 us: per_device(): pl.pallas_call(functools.partial(kernel, shape_xy), out_shape=(pltpu.VMEM...]
where the time goes in v1:
time: 32.9 us; the launch traced here: 32.8 us
  Pallas kernels  32.1 us (98%)
  between operations  0.64 us (2%)
    pallas_call x1, Pallas kernels, per_device(): pl.pallas_call(functools.partial(kernel, shape_xy), out_shape=(pltpu.VMEM...  31.2 us
    pallas_call x1, Pallas kernels, per_device(): pl.pallas_call(deliver, out_shape=(pltpu.HBM(args[0].shape, F32),) * 3, i...  0.93 us

profile of v1, /device:TPU:7, one launch (start us, length us, event | category | flops | bytes accessed | tf_op | source)
XLA Modules:
  0.0 32.8 jit_solution(9527222799106217435)
XLA Ops:
  0.6 31.2 %shard_map.94 = (f32[8,64,128]{2,1,0:T(8,128)S(1)}, f32[8,64,128]{2,1,0:T(8,128)S(1)}, f32[8,64,128]{2,1,0:T(8,128)S(1)}) custom-call(f32[16,32,128]{2,1,0:T(8,128)} %up_ref.1, f32[16,32,128]{2,1,0:T(8,128)} %uc_ref.1, f32[16,32,128]{2,1,0:T(8,128)} %an_ref.1, f32[16,32,128]{2,1,0:T(8,128)} %ac_ref.1, f32[16,32,128]{2,1,0:T(8,128)} %im_ref.1, ...), custom_call_target="tpu_custom_call" | custom-call | tf_op jit(solution)/shard_map/pallas_call | solution.py:723
  31.9 0.9 %shard_map.95 = (f32[16,32,128]{2,1,0:T(8,128)}, f32[16,32,128]{2,1,0:T(8,128)}, f32[16,32,128]{2,1,0:T(8,128)}) custom-call(f32[8,64,128]{2,1,0:T(8,128)S(1)} %get-tuple-element.6.refs_0_, f32[8,64,128]{2,1,0:T(8,128)S(1)} %get-tuple-element.7.refs_1_, f32[8,64,128]{2,1,0:T(8,128)S(1)} %get-tuple-element.8.refs_2_), custom_call_target="tpu_custom_call" | custom-call | tf_op jit(solution)/shard_map/pallas_call | solution.py:781

commit v2 on v1

--- a/solution.py
+++ b/solution.py
@@ -135,8 +135,6 @@
     xr0,
     yr0,
     dr0,
-    xr1,
-    yr1,
     xrk,
     yrk,
     xs,
@@ -186,8 +184,12 @@
     targets_y = [target_y(0), target_y(1)]
     targets_d = [target_d(0, 0), target_d(0, 1), target_d(1, 0), target_d(1, 1)]
 
+    barrier = pltpu.get_barrier_semaphore()
+    for device, _ in targets_x + targets_y + targets_d:
+        pl.semaphore_signal(barrier, inc=1, device_id=device, device_id_type=MESH)
+
     loads = []
-    for k, ref in enumerate((id_ref, im_ref, uc_ref, up_ref, ac_ref, an_ref)):
+    for k, ref in enumerate((id_ref, uc_ref, im_ref, up_ref, ac_ref, an_ref)):
         for half in range(2):
             loads.append(
                 pltpu.make_async_copy(
@@ -199,9 +201,6 @@
     loads.append(pltpu.make_async_copy(fm_ref, mask, in_sem.at[12]))
     for load in loads:
         load.start()
-    barrier = pltpu.get_barrier_semaphore()
-    for device, _ in targets_x + targets_y + targets_d:
-        pl.semaphore_signal(barrier, inc=1, device_id=device, device_id_type=MESH)
 
     sub = lax.broadcasted_iota(jnp.int32, (8, LANES), 0)
     lane = lax.broadcasted_iota(jnp.int32, (8, LANES), 1)
@@ -220,24 +219,6 @@
         after = pltpu.roll(values, LANES - 1, values.ndim - 1)
         return values + jnp.where(z_low, before, jnp.where(z_high, after, 0.0))
 
-    tiles = [zero, zero]
-    for i in range(8):
-        for j in range(8):
-            value = F32(DERIVATIVE[i, j])
-            tiles[0] = jnp.where(jnp.logical_and(sub == j, zplace == i), value, tiles[0])
-            tiles[1] = jnp.where(jnp.logical_and(sub == i, zplace == j), value, tiles[1])
-    for which in range(2):
-        rows = [jnp.where(lane // 8 == k, tiles[which], 0.0) for k in range(LANES // 8)]
-        if which == 1:
-            rows = [sum_third(row) for row in rows]
-        block = jnp.concatenate(rows, axis=0)
-        high = block.astype(BF16)
-        low = (block - high.astype(F32)).astype(BF16)
-        for half in range(2):
-            here = slice(LANES * half, LANES * half + LANES)
-            table[which, here, :LANES] = high
-            table[which, here, LANES:] = low
-
     def one_if(flag):
         return jnp.where(flag, 1, 0)
 
@@ -292,16 +273,11 @@
 
     def copies(src, dst, ssem, rsem, first):
         out = []
-        for side in range(2):
-            device, slot = targets_x[side]
-            out.append((src[0].at[side], dst[0].at[slot], side, slot, device))
-        for side in range(2):
-            device, slot = targets_y[side]
-            out.append((src[1].at[side], dst[1].at[slot], 2 + side, 2 + slot, device))
-        if len(src) > 2:
-            for k in range(4):
-                device, slot = targets_d[k]
-                out.append((src[2], dst[2].at[slot], 4 + k, 4 + slot, device))
+        for kind, targets in ((2, targets_d), (1, targets_y), (0, targets_x)):
+            if src[kind] is not None:
+                for k, (device, slot) in enumerate(targets):
+                    a = src[kind] if kind == 2 else src[kind].at[k]
+                    out.append((a, dst[kind].at[slot], 2 * kind + k, 2 * kind + slot, device))
         for a, b, i, j, device in out:
             pltpu.make_async_remote_copy(
                 src_ref=a,
@@ -312,26 +288,24 @@
                 device_id_type=MESH,
             ).start()
 
-    def arrive(src, dst, ssem, rsem, first, which=range(8)):
-        pairs = [(src[0].at[side], dst[0].at[side]) for side in range(2)]
-        pairs += [(src[1].at[side], dst[1].at[side]) for side in range(2)]
-        if len(src) > 2:
-            pairs += [(src[2], dst[2].at[k]) for k in range(4)]
-        for i, (a, b) in enumerate(pairs):
-            if i in which:
-                copy = pltpu.make_async_remote_copy(
-                    src_ref=a,
-                    dst_ref=b,
-                    send_sem=ssem.at[first + i],
-                    recv_sem=rsem.at[first + i],
-                    device_id=targets_x[0][0],
-                    device_id_type=MESH,
-                )
-                copy.wait_recv()
-                copy.wait_send()
-
-    homes = (cz, scale, keep, uf, vf.at[1], aa.at[8], va)
-    groups = ((0, 1, 2), (3, 4), (5, 6))
+    def arrive(src, dst, ssem, rsem, first):
+        for kind in range(3):
+            if src[kind] is not None:
+                for k in range(4 if kind == 2 else 2):
+                    copy = pltpu.make_async_remote_copy(
+                        src_ref=src[kind] if kind == 2 else src[kind].at[k],
+                        dst_ref=dst[kind].at[k],
+                        send_sem=ssem.at[first + 2 * kind + k],
+                        recv_sem=rsem.at[first + 2 * kind + k],
+                        device_id=targets_x[0][0],
+                        device_id_type=MESH,
+                    )
+                    copy.wait_recv()
+                    copy.wait_send()
+
+    homes = (cz, uf, scale, keep, vf.at[1], aa.at[8], va)
+    places = (0, 1, 2, None, 3, 4, 5)
+    groups = ((0, 1), (2, 3, 4), (5, 6))
 
     def natural(k, ix, iy):
         return nat[k, ix, pl.ds(iy, 8, stride=8), :]
@@ -354,46 +328,77 @@
             value = value * half_y_high
         return value
 
-    for load in loads[0:2]:
-        load.wait()
-    for ix in range(8):
-        for iy in range(8):
-            raw = natural(0, ix, iy) * (wz * float(GLL_WEIGHTS[ix] * GLL_WEIGHTS[iy]))
-            summed = sum_third(raw)
-            cz[ix, iy] = raw
-            cx[ix, iy] = summed
-            cy[ix, iy] = summed
-    for load in loads[2:4]:
-        load.wait()
-    for ix in range(8):
-        for iy in range(8):
-            raw = natural(1, ix, iy) * (wz * float(GLL_WEIGHTS[ix] * GLL_WEIGHTS[iy]))
-            scale[ix, iy] = sum_third(raw)
-    loads[12].wait()
-    spread = jnp.where(
-        lax.broadcasted_iota(jnp.int32, (16, LANES), 1) // 8
-        == lax.broadcasted_iota(jnp.int32, (16, LANES), 0),
-        1.0,
-        0.0,
-    ).astype(F32)
-    faces = []
-    for f in range(6):
-        cells = jnp.concatenate([mask[f, 0], mask[f, 1]], axis=0).astype(F32)
-        faces.append(jnp.dot(cells, spread, preferred_element_type=F32))
-    third_face = sum_third(jnp.where(zplace == 0, faces[4], jnp.where(zplace == 7, faces[5], 0.0)))
-    faces = [sum_third(wz * face) for face in faces[:4]]
-    for ix in range(8):
-        for iy in range(8):
-            value = third_face * float(GLL_WEIGHTS[ix] * GLL_WEIGHTS[iy])
-            if ix == 0:
-                value = value + faces[0] * float(GLL_WEIGHTS[iy])
-            if ix == 7:
-                value = value + faces[1] * float(GLL_WEIGHTS[iy])
-            if iy == 0:
-                value = value + faces[2] * float(GLL_WEIGHTS[ix])
-            if iy == 7:
-                value = value + faces[3] * float(GLL_WEIGHTS[ix])
-            keep[ix, iy] = value
+    def fill_tables():
+        tiles = [zero, zero]
+        for i in range(8):
+            for j in range(8):
+                value = F32(DERIVATIVE[i, j])
+                tiles[0] = jnp.where(jnp.logical_and(sub == j, zplace == i), value, tiles[0])
+                tiles[1] = jnp.where(jnp.logical_and(sub == i, zplace == j), value, tiles[1])
+        for which in range(2):
+            rows = [jnp.where(lane // 8 == k, tiles[which], 0.0) for k in range(LANES // 8)]
+            if which == 1:
+                rows = [sum_third(row) for row in rows]
+            block = jnp.concatenate(rows, axis=0)
+            high = block.astype(BF16)
+            low = (block - high.astype(F32)).astype(BF16)
+            for half in range(2):
+                here = slice(LANES * half, LANES * half + LANES)
+                table[which, here, :LANES] = high
+                table[which, here, LANES:] = low
+
+    faces_at = [(ix, iy) for ix in range(8) for iy in range(8) if ix in (0, 7) or iy in (0, 7)]
+    inside_at = [(ix, iy) for ix in range(1, 7) for iy in range(1, 7)]
+    face_parts = ((0,), (7,), (slice(1, 7), 0), (slice(1, 7), 7))
+    inside = (slice(1, 7), slice(1, 7))
+
+    def arrived_here(f):
+        for load in loads[2 * places[f] : 2 * places[f] + 2]:
+            load.wait()
+
+    def fill(f, nodes):
+        for ix, iy in nodes:
+            weight = float(GLL_WEIGHTS[ix] * GLL_WEIGHTS[iy])
+            if f == 0:
+                raw = natural(0, ix, iy) * (wz * weight)
+                summed = sum_third(raw)
+                cz[ix, iy] = raw
+                cx[ix, iy] = summed
+                cy[ix, iy] = summed
+            elif f == 2:
+                scale[ix, iy] = sum_third(natural(2, ix, iy) * (wz * weight))
+            elif f == 3:
+                value = third_face * weight
+                if ix == 0:
+                    value = value + faces[0] * float(GLL_WEIGHTS[iy])
+                if ix == 7:
+                    value = value + faces[1] * float(GLL_WEIGHTS[iy])
+                if iy == 0:
+                    value = value + faces[2] * float(GLL_WEIGHTS[ix])
+                if iy == 7:
+                    value = value + faces[3] * float(GLL_WEIGHTS[ix])
+                keep[ix, iy] = value
+            else:
+                homes[f][ix, iy] = sum_third(natural(places[f], ix, iy) * share(ix, iy))
+
+    def damping_faces():
+        spread = jnp.where(
+            lax.broadcasted_iota(jnp.int32, (16, LANES), 1) // 8
+            == lax.broadcasted_iota(jnp.int32, (16, LANES), 0),
+            1.0,
+            0.0,
+        ).astype(F32)
+        cells = [
+            jnp.dot(
+                jnp.concatenate([mask[f, 0], mask[f, 1]], axis=0).astype(F32),
+                spread,
+                preferred_element_type=F32,
+            )
+            for f in range(6)
+        ]
+        ends = jnp.where(zplace == 0, cells[4], jnp.where(zplace == 7, cells[5], 0.0))
+        return [sum_third(wz * cell) for cell in cells[:4]], sum_third(ends)
+
     def join_first(home):
         first, last = join_x(home[0], home[7])
         home[0] = first
@@ -406,8 +411,9 @@
 
     def pack_field(f):
         home = homes[f]
-        join_first(home)
-        join_second(home)
+        if f > 0:
+            join_first(home)
+            join_second(home)
         xs0[0, f], xs0[1, f] = pack_x(home[0], home[7])
         ys0[0, f], ys0[1, f] = pack_y(home[:, 0], home[:, 7])
         ds0[f] = corner_lines(home[0, 0], home[0, 7], home[7, 0], home[7, 7])
@@ -419,81 +425,109 @@
         return src, dst, send0, recv0, 8 * g
 
     for f in groups[0]:
+        arrived_here(f)
+        fill(f, faces_at)
         pack_field(f)
-    join_first(cy)
-    join_second(cx)
-    one_sided = ((xs1, ys1), (xr1, yr1), send0, recv0, 24)
-    xs1[0], xs1[1] = pack_x(cy[0], cy[7])
-    ys1[0], ys1[1] = pack_y(cx[:, 0], cx[:, 7])
+    loads[12].wait()
+    faces, third_face = damping_faces()
+    for f in groups[1]:
+        if f != 3:
+            arrived_here(f)
+        fill(f, faces_at)
+        pack_field(f)
     pl.semaphore_wait(barrier, 8)
-    copies(*one_sided)
     copies(*group_refs(0))
-
-    for g in (1, 2):
-        for f in groups[g]:
-            k = f - 1
-            for load in loads[2 * k : 2 * k + 2]:
-                load.wait()
-            home = homes[f]
-            for ix in range(8):
-                for iy in range(8):
-                    home[ix, iy] = sum_third(natural(k, ix, iy) * share(ix, iy))
-            pack_field(f)
-        copies(*group_refs(g))
-
-    def add_x(home, received):
-        for side, node in ((0, 0), (1, 7)):
-            home[node] = home[node] + jnp.where(halo_x[side], unpack_x(side, received[side]), 0.0)
-
-    def add_y(home, received):
-        for side, node in ((0, 0), (1, 7)):
-            part = jnp.where(halo_y[side], unpack_y(side, received[side]), 0.0)
-            home[:, node] = home[:, node] + part
-
-    def add_field(f):
-        home = homes[f]
-        add_x(home, xr0.at[:, f])
-        add_y(home, yr0.at[:, f])
-        for k, (ix, iy, _, turn) in enumerate(node_d):
-            home[ix, iy] = home[ix, iy] + jnp.where(halo_d[k], roll_sub(dr0[k, f], turn), 0.0)
-
-    arrive(*one_sided)
-    add_x(cy, xr1)
-    add_y(cx, yr1)
-
-    end_x = [
-        jnp.where(low_x, F32(DERIVATIVE[i, 0]), F32(DERIVATIVE[i, 7])) for i in range(8)
-    ]
-    end_y = [
-        jnp.where(ey < 2, F32(DERIVATIVE[i, 0]), F32(DERIVATIVE[i, 7])) for i in range(8)
-    ]
-    for c in range(0, 8, CHUNK):
-        here = slice(c, c + CHUNK)
+    copies(*group_refs(1))
+    for home, joins in ((cz, (join_first, join_second)), (cy, (join_first,)), (cx, (join_second,))):
+        for join in joins:
+            join(home)
+
+    def rates(here):
+        one_over = 1.0 / scale[here]
+        scale[here] = (TIME_STEP * TIME_STEP) * one_over
+        keep[here] = 1.0 - TIME_STEP * keep[here] * one_over
+
+    end_x = [jnp.where(low_x, F32(DERIVATIVE[i, 0]), F32(DERIVATIVE[i, 7])) for i in range(8)]
+    end_y = [jnp.where(ey < 2, F32(DERIVATIVE[i, 0]), F32(DERIVATIVE[i, 7])) for i in range(8)]
+
+    def fill_rows(here):
         rows = apply_eight([end_x[i] * cx[i, here] for i in range(8)], BACKWARD)
         for j in range(8):
             kx[j, here] = rows[j]
         rows = apply_eight([end_y[i] * cy[here, i] for i in range(8)], BACKWARD)
         for j in range(8):
             ky[here, j] = rows[j]
+
+    for f in range(5):
+        fill(f, inside_at)
+    fill_tables()
+    rates(inside)
+    vf[1, 1:7, 1:7] = uf[inside] - vf[1, 1:7, 1:7]
+    for c in range(1, 7, CHUNK):
+        fill_rows(slice(c, c + CHUNK))
+
+    for f in groups[2]:
+        arrived_here(f)
+        fill(f, faces_at)
+        pack_field(f)
+    copies(*group_refs(2))
+    for f in groups[2]:
+        fill(f, inside_at)
+    va[inside] = aa[8, 1:7, 1:7] - va[inside]
+
+    def from_sides(f):
+        parts_x = [jnp.where(halo_x[s], unpack_x(s, xr0[s, f]), 0.0) for s in range(2)]
+        parts_y = [jnp.where(halo_y[s], unpack_y(s, yr0[s, f]), 0.0) for s in range(2)]
+        return parts_x, parts_y
+
+    def add_x(home, parts):
+        for node, part in zip((0, 7), parts):
+            home[node] = home[node] + part
+
+    def add_y(home, parts):
+        for node, part in zip((0, 7), parts):
+            home[:, node] = home[:, node] + part
+
+    def add_field(f):
+        home = homes[f]
+        parts_x, parts_y = from_sides(f)
+        add_x(home, parts_x)
+        add_y(home, parts_y)
+        if f == 0:
+            add_x(cy, [sum_third(part) for part in parts_x])
+            add_y(cx, [sum_third(part) for part in parts_y])
+            for node, part in zip((0, 7), parts_x):
+                first, last = join_y(part[0], part[7])
+                cz[node, 0] = cz[node, 0] + (first - part[0])
+                cz[node, 7] = cz[node, 7] + (last - part[7])
+            for node, part in zip((0, 7), parts_y):
+                first, last = join_x(part[0], part[7])
+                cz[0, node] = cz[0, node] + (first - part[0])
+                cz[7, node] = cz[7, node] + (last - part[7])
+        for k, (ix, iy, _, turn) in enumerate(node_d):
+            home[ix, iy] = home[ix, iy] + jnp.where(halo_d[k], roll_sub(dr0[k, f], turn), 0.0)
+
+    arrive(*group_refs(0))
+    add_field(0)
+    for c in (0, 7):
+        fill_rows(slice(c, c + 1))
+
     def put_faces(side_x, side_y, fx0, fx1, fy0, fy1):
         side_x[0], side_x[1] = pack_x(fx0, fx1)
         side_y[0], side_y[1] = pack_y(fy0, fy1)
 
-    ends = ((xs1, ys1), (xrk, yrk), sendk, recvk, 0)
+    ends = ((xs1, ys1, None), (xrk, yrk, None), sendk, recvk, 0)
     put_faces(xs1, ys1, kx[0], kx[7], ky[:, 0], ky[:, 7])
     copies(*ends)
-    arrive(*group_refs(0))
-    for f in groups[0]:
-        add_field(f)
-    for ix in range(8):
-        one_over = 1.0 / scale[ix]
-        scale[ix] = (TIME_STEP * TIME_STEP) * one_over
-        keep[ix] = 1.0 - TIME_STEP * keep[ix] * one_over
-    arrive(*group_refs(1))
-    for f in groups[1]:
-        add_field(f)
-    for ix in range(8):
-        vf[1, ix] = uf[ix] - vf[1, ix]
+    add_field(1)
+
+    def rest_of_setup():
+        arrive(*group_refs(1))
+        for f in groups[1]:
+            add_field(f)
+        for here in face_parts:
+            rates(here)
+            vf[(1, *here)] = uf[here] - vf[(1, *here)]
 
     def times(values, which):
         high = values.astype(BF16)
@@ -503,7 +537,7 @@
         )
         return both[:, :LANES] + both[:, LANES:]
 
-    def advance(source, gradient, v_from, u_to, v_to):
+    def advance(source, gradient, v_from, u_to, v_to, between=None):
         slope = times(source[...].reshape(512, LANES), 0)
         gradient[2] = slope.reshape(8, 8, 8, LANES)
         acc[...] = times(cz[...].reshape(512, LANES) * slope, 1).reshape(8, 8, 8, LANES)
@@ -516,6 +550,8 @@
             image[0], image[7] = join_x(image[0], image[7])
             for j in range(8):
                 acc[j, here] = acc[j, here] + image[j]
+        if between is not None:
+            between()
         for c in range(0, 8, CHUNK):
             here = slice(c, c + CHUNK)
             now = [source[here, j] for j in range(8)]
@@ -537,28 +573,44 @@
         return along_x, along_y
 
     def mail(kind, field, slot):
-        src = [xs.at[kind, field, slot], ys.at[kind, field, slot]]
-        dst = [xr.at[kind, field, slot], yr.at[kind, field, slot]]
-        if kind == 0:
-            src.append(ds.at[field, slot])
-            dst.append(dr.at[field, slot])
-        return src, dst, send.at[field, slot], recv.at[field, slot], 8 * kind
-
-    def begin(field, turn, source, gradient, v_from, u_to, v_to):
+        if kind < 2:
+            src = (xs.at[kind, field, slot], ys.at[kind, field, slot], None)
+            dst = (xr.at[kind, field, slot], yr.at[kind, field, slot], None)
+        else:
+            src = (None, None, ds.at[field, slot])
+            dst = (None, None, dr.at[field, slot])
+        return src, dst, send.at[field, slot], recv.at[field, slot], (0, 8, 0)[kind]
+
+    def begin(field, turn, source, gradient, v_from, u_to, v_to, between=None):
         slot = lax.rem(turn, 2)
         first, second = mail(0, field, slot), mail(1, field, slot)
+        corners = mail(2, field, slot)
         own_x, own_y = face_rows(source)
         put_faces(first[0][0], first[0][1], own_x, own_x, own_y, own_y)
-        for side, node in ((0, 0), (1, 7)):
-            sp_x[field, side] = scale[node] * own_x
-            sp_y[field, side] = scale[:, node] * own_y
-        lines_x = [jnp.sum(kx[:, n] * sp_y[field, s], axis=0) for s, n in ((0, 0), (1, 7))]
-        lines_y = [jnp.sum(ky[n] * sp_x[field, s], axis=0) for s, n in ((0, 0), (1, 7))]
-        ds[field, slot] = -(
-            jnp.where(ey == 0, lines_x[0], lines_x[1]) + jnp.where(low_x, lines_y[0], lines_y[1])
-        )
         copies(*first)
-        advance(source, gradient, v_from, u_to, v_to)
+
+        def send_corners():
+            for side, node in ((0, 0), (1, 7)):
+                sp_x[field, side] = scale[node] * own_x
+                sp_y[field, side] = scale[:, node] * own_y
+            lines_x = [jnp.sum(kx[:, n] * sp_y[field, s], axis=0) for s, n in ((0, 0), (1, 7))]
+            lines_y = [jnp.sum(ky[n] * sp_x[field, s], axis=0) for s, n in ((0, 0), (1, 7))]
+            ds[field, slot] = -(
+                jnp.where(ey == 0, lines_x[0], lines_x[1])
+                + jnp.where(low_x, lines_y[0], lines_y[1])
+            )
+            copies(*corners)
+
+        if between is None:
+            send_corners()
+            advance(source, gradient, v_from, u_to, v_to)
+        else:
+
+            def both():
+                between()
+                send_corners()
+
+            advance(source, gradient, v_from, u_to, v_to, both)
         next_x, next_y = face_rows(u_to)
         put_faces(second[0][0], second[0][1], next_x, next_x, next_y, next_y)
         copies(*second)
@@ -575,7 +627,7 @@
 
     def complete(field, turn, u, v):
         letter = mail(0, field, lax.rem(turn, 2))
-        arrive(*letter, range(4))
+        arrive(*letter)
         from_x, from_y = letter[1][:2]
         mend(
             u,
@@ -587,9 +639,9 @@
     def finish(field, turn, source, gradient, v_from, u_to, v_to):
         slot = lax.rem(turn, 2)
         advance(source, gradient, v_from, u_to, v_to)
-        first, second = mail(0, field, slot), mail(1, field, slot)
+        second, corners = mail(1, field, slot), mail(2, field, slot)
         arrive(*second)
-        from_x, from_y = second[1]
+        from_x, from_y = second[1][:2]
         parts_x, parts_y = [], []
         for s in range(2):
             part = unpack_x(s, from_x[s]) - kn_x[s] * sp_x[field, s]
@@ -597,17 +649,17 @@
             part = unpack_y(s, from_y[s]) - kn_y[s] * sp_y[field, s]
             parts_y.append(jnp.where(halo_y[s], part, 0.0))
         mend(u_to, v_to, parts_x, parts_y)
-        arrive(*first, range(4, 8))
-        from_d = first[1][2]
+        arrive(*corners)
+        from_d = corners[1][2]
         for k, (ix, iy, _, turn_by) in enumerate(node_d):
             line = jnp.where(halo_d[k], roll_sub(from_d[k], turn_by), 0.0)
             part = scale[ix, iy] * line
             u_to[ix, iy] = u_to[ix, iy] - part
             v_to[ix, iy] = v_to[ix, iy] - part
 
-    def begin_u(turn):
+    def begin_u(turn, between=None):
         n = 2 * turn + 1
-        begin(0, turn, uf, gu.at[n], vf.at[n], uf, vf.at[n + 1])
+        begin(0, turn, uf, gu.at[n], vf.at[n], uf, vf.at[n + 1], between)
 
     def begin_a(turn):
         n = 8 - 2 * turn
@@ -623,12 +675,12 @@
         complete(1, turn, aa.at[n], va)
         finish(1, turn, aa.at[n], ga.at[n], va, aa.at[n - 1], va)
 
-    begin_u(0)
+    begin_u(0, rest_of_setup)
     arrive(*group_refs(2))
     for f in groups[2]:
         add_field(f)
-    for ix in range(8):
-        va[ix] = aa[8, ix] - va[ix]
+    for here in face_parts:
+        va[here] = aa[(8, *here)] - va[here]
     begin_a(0)
     arrive(*ends)
     for side in range(2):
@@ -667,9 +719,12 @@
 
     last = STEPS // 2 - 1
     finish_u(last)
+    for ix in range(8):
+        sums[0, ix] = sums[0, ix] + density_of((8,), ix)
+        modulus, impedance = moduli_of((7, 8), ix)
+        sums[1, ix] = sums[1, ix] + modulus
+        sums[2, ix] = sums[2, ix] + impedance
     complete(1, last, aa.at[1], va)
-    arrive(*mail(0, 1, last % 2), range(4, 8))
-    arrive(*mail(1, 1, last % 2))
     source, gradient = aa.at[1], ga.at[1]
     gradient[2] = times(source[...].reshape(512, LANES), 0).reshape(8, 8, 8, LANES)
     for c in range(0, 8, CHUNK):
@@ -682,8 +737,8 @@
             gradient[1, here, j] = slopes[j]
 
     for ix in range(8):
-        density = sums[0, ix] + density_of((1, 8), ix)
-        modulus, impedance = moduli_of((1, 7, 8), ix)
+        density = sums[0, ix] + density_of((1,), ix)
+        modulus, impedance = moduli_of((1,), ix)
         modulus = sums[1, ix] + modulus
         impedance = (sums[2, ix] + impedance) * (1.0 - keep[ix])
         for iy in range(8):
@@ -692,6 +747,8 @@
             dens_ref[ix, rows, :] = weight * density[iy]
             mod_ref[ix, rows, :] = modulus[iy]
             imp_ref[ix, rows, :] = impedance[iy]
+    arrive(*mail(2, 1, last % 2))
+    arrive(*mail(1, 1, last % 2))
 
 
 def deliver(*refs):
@@ -758,8 +815,6 @@
             vectors(4, 7),
             vectors(2, 4),
             vectors(2, 2),
-            vectors(2, 4),
-            vectors(2, 2),
             vectors(2, 2, 2, 2, 4),
             vectors(2, 2, 2, 2, 2),
             vectors(2, 2),
@@ -767,8 +822,8 @@
             vectors(2, 2, 2, 2, 2),
             vectors(2, 2, 4),
             pltpu.SemaphoreType.DMA((13,)),
-            pltpu.SemaphoreType.DMA((28,)),
-            pltpu.SemaphoreType.DMA((28,)),
+            pltpu.SemaphoreType.DMA((24,)),
+            pltpu.SemaphoreType.DMA((24,)),
             pltpu.SemaphoreType.DMA((4,)),
             pltpu.SemaphoreType.DMA((4,)),
             pltpu.SemaphoreType.DMA((2, 2, 12)),

time: 32.9 us -> 31.8 us (0.967)
  Pallas kernels: 32.1 us -> 31.1 us
    pallas_call x1, Pallas kernels: 31.2 us -> 30.1 us  [per_device(): pl.pallas_call(functools.partial(kernel, shape_xy), out_shape=(pltpu.VMEM...]
where the time goes in v2:
time: 31.8 us; the launch traced here: 31.7 us
  Pallas kernels  31.1 us (98%)
  between operations  0.64 us (2%)
    pallas_call x1, Pallas kernels, per_device(): pl.pallas_call(functools.partial(kernel, shape_xy), out_shape=(pltpu.VMEM...  30.1 us
    pallas_call x1, Pallas kernels, per_device(): pl.pallas_call(deliver, out_shape=(pltpu.HBM(args[0].shape, F32),) * 3, i...  0.93 us

profile of v2, /device:TPU:7, one launch (start us, length us, event | category | flops | bytes accessed | tf_op | source)
XLA Modules:
  0.0 31.7 jit_solution(11785874680510602095)
XLA Ops:
  0.6 30.1 %shard_map.94 = (f32[8,64,128]{2,1,0:T(8,128)S(1)}, f32[8,64,128]{2,1,0:T(8,128)S(1)}, f32[8,64,128]{2,1,0:T(8,128)S(1)}) custom-call(f32[16,32,128]{2,1,0:T(8,128)} %up_ref.1, f32[16,32,128]{2,1,0:T(8,128)} %uc_ref.1, f32[16,32,128]{2,1,0:T(8,128)} %an_ref.1, f32[16,32,128]{2,1,0:T(8,128)} %ac_ref.1, f32[16,32,128]{2,1,0:T(8,128)} %im_ref.1, ...), custom_call_target="tpu_custom_call" | custom-call | tf_op jit(solution)/shard_map/pallas_call | solution.py:780
  30.8 0.9 %shard_map.95 = (f32[16,32,128]{2,1,0:T(8,128)}, f32[16,32,128]{2,1,0:T(8,128)}, f32[16,32,128]{2,1,0:T(8,128)}) custom-call(f32[8,64,128]{2,1,0:T(8,128)S(1)} %get-tuple-element.6.refs_0_, f32[8,64,128]{2,1,0:T(8,128)S(1)} %get-tuple-element.7.refs_1_, f32[8,64,128]{2,1,0:T(8,128)S(1)} %get-tuple-element.8.refs_2_), custom_call_target="tpu_custom_call" | custom-call | tf_op jit(solution)/shard_map/pallas_call | solution.py:836

commit v3 on v2

--- a/solution.py
+++ b/solution.py
@@ -127,27 +127,17 @@
     kn_x,
     kn_y,
     sums,
-    xs0,
-    ys0,
-    ds0,
-    xs1,
-    ys1,
-    xr0,
-    yr0,
-    dr0,
-    xrk,
-    yrk,
-    xs,
-    ys,
-    ds,
-    xr,
-    yr,
-    dr,
+    outs0,
+    lines0,
+    ins0,
+    ends_out,
+    ends_in,
+    outs,
+    lines,
+    ins,
     in_sem,
     send0,
     recv0,
-    sendk,
-    recvk,
     send,
     recv,
 ):
@@ -185,7 +175,7 @@
     targets_d = [target_d(0, 0), target_d(0, 1), target_d(1, 0), target_d(1, 1)]
 
     barrier = pltpu.get_barrier_semaphore()
-    for device, _ in targets_x + targets_y + targets_d:
+    for device, _ in targets_d + targets_y + targets_x:
         pl.semaphore_signal(barrier, inc=1, device_id=device, device_id_type=MESH)
 
     loads = []
@@ -230,7 +220,7 @@
         jnp.logical_and(halo_x[1], halo_y[0]),
         jnp.logical_and(halo_x[1], halo_y[1]),
     ]
-    node_d = ((0, 0, 0, 1), (0, 7, 3, -1), (7, 0, 4, 1), (7, 7, 7, -1))
+    node_d = ((0, 0, 1), (0, 7, -1), (7, 0, 1), (7, 7, -1))
 
     def join_x(first, last):
         return (
@@ -271,37 +261,46 @@
     def corner_lines(n00, n07, n70, n77):
         return jnp.where(low_x, jnp.where(ey == 0, n00, n07), jnp.where(ey == 0, n70, n77))
 
-    def copies(src, dst, ssem, rsem, first):
-        out = []
-        for kind, targets in ((2, targets_d), (1, targets_y), (0, targets_x)):
-            if src[kind] is not None:
-                for k, (device, slot) in enumerate(targets):
-                    a = src[kind] if kind == 2 else src[kind].at[k]
-                    out.append((a, dst[kind].at[slot], 2 * kind + k, 2 * kind + slot, device))
-        for a, b, i, j, device in out:
-            pltpu.make_async_remote_copy(
-                src_ref=a,
-                dst_ref=b,
-                send_sem=ssem.at[first + i],
-                recv_sem=rsem.at[first + j],
-                device_id=device,
-                device_id_type=MESH,
-            ).start()
-
-    def arrive(src, dst, ssem, rsem, first):
-        for kind in range(3):
-            if src[kind] is not None:
-                for k in range(4 if kind == 2 else 2):
-                    copy = pltpu.make_async_remote_copy(
-                        src_ref=src[kind] if kind == 2 else src[kind].at[k],
-                        dst_ref=dst[kind].at[k],
-                        send_sem=ssem.at[first + 2 * kind + k],
-                        recv_sem=rsem.at[first + 2 * kind + k],
-                        device_id=targets_x[0][0],
-                        device_id_type=MESH,
-                    )
-                    copy.wait_recv()
-                    copy.wait_send()
+    def copy(src, dst, ssem, rsem, device):
+        return pltpu.make_async_remote_copy(
+            src_ref=src,
+            dst_ref=dst,
+            send_sem=ssem,
+            recv_sem=rsem,
+            device_id=device,
+            device_id_type=MESH,
+        )
+
+    def post_faces(out, into, ssem, rsem, lead=()):
+        for side, (device, slot) in enumerate(targets_y):
+            src, dst = out.at[(*lead, pl.ds(8 + 2 * side, 2))], into.at[(*lead, pl.ds(8 + 2 * slot, 2))]
+            copy(src, dst, ssem, rsem, device).start()
+        for side, (device, slot) in enumerate(targets_x):
+            src, dst = out.at[(*lead, pl.ds(4 * side, 4))], into.at[(*lead, pl.ds(4 * slot, 4))]
+            copy(src, dst, ssem, rsem, device).start()
+
+    def post_lines(line, into, ssem, rsem, lead=()):
+        for device, slot in targets_d:
+            copy(line, into.at[(*lead, 12 + slot)], ssem, rsem, device).start()
+
+    def received(into, rsem):
+        copy(into, into, rsem, rsem, targets_x[0][0]).wait_recv()
+
+    def sent(out, ssem):
+        copy(out, out, ssem, ssem, targets_x[0][0]).wait_send()
+
+    def put_faces(out, fx0, fx1, fy0, fy1):
+        out[0:4], out[4:8] = pack_x(fx0, fx1)
+        out[8:10], out[10:12] = pack_y(fy0, fy1)
+
+    def read_x(into, side):
+        return jnp.where(halo_x[side], unpack_x(side, into[4 * side : 4 * side + 4]), 0.0)
+
+    def read_y(into, side):
+        return jnp.where(halo_y[side], unpack_y(side, into[8 + 2 * side : 10 + 2 * side]), 0.0)
+
+    def read_line(into, k):
+        return jnp.where(halo_d[k], roll_sub(into[12 + k], node_d[k][2]), 0.0)
 
     homes = (cz, uf, scale, keep, vf.at[1], aa.at[8], va)
     places = (0, 1, 2, None, 3, 4, 5)
@@ -414,15 +413,18 @@
         if f > 0:
             join_first(home)
             join_second(home)
-        xs0[0, f], xs0[1, f] = pack_x(home[0], home[7])
-        ys0[0, f], ys0[1, f] = pack_y(home[:, 0], home[:, 7])
-        ds0[f] = corner_lines(home[0, 0], home[0, 7], home[7, 0], home[7, 7])
-
-    def group_refs(g):
+        put_faces(outs0.at[f], home[0], home[7], home[:, 0], home[:, 7])
+        lines0[f] = corner_lines(home[0, 0], home[0, 7], home[7, 0], home[7, 7])
+
+    def post_group(g):
         here = pl.ds(groups[g][0], len(groups[g]))
-        src = (xs0.at[:, here], ys0.at[:, here], ds0.at[here])
-        dst = (xr0.at[:, here], yr0.at[:, here], dr0.at[:, here])
-        return src, dst, send0, recv0, 8 * g
+        every = (pl.ds(0, len(groups[g])),)
+        out, into = outs0.at[here], ins0.at[here]
+        post_lines(lines0.at[here], into, send0.at[g], recv0.at[g], every)
+        post_faces(out, into, send0.at[g], recv0.at[g], every)
+
+    def receive_group(g):
+        received(ins0.at[pl.ds(groups[g][0], len(groups[g]))], recv0.at[g])
 
     for f in groups[0]:
         arrived_here(f)
@@ -436,8 +438,8 @@
         fill(f, faces_at)
         pack_field(f)
     pl.semaphore_wait(barrier, 8)
-    copies(*group_refs(0))
-    copies(*group_refs(1))
+    post_group(0)
+    post_group(1)
     for home, joins in ((cz, (join_first, join_second)), (cy, (join_first,)), (cx, (join_second,))):
         for join in joins:
             join(home)
@@ -470,16 +472,11 @@
         arrived_here(f)
         fill(f, faces_at)
         pack_field(f)
-    copies(*group_refs(2))
+    post_group(2)
     for f in groups[2]:
         fill(f, inside_at)
     va[inside] = aa[8, 1:7, 1:7] - va[inside]
 
-    def from_sides(f):
-        parts_x = [jnp.where(halo_x[s], unpack_x(s, xr0[s, f]), 0.0) for s in range(2)]
-        parts_y = [jnp.where(halo_y[s], unpack_y(s, yr0[s, f]), 0.0) for s in range(2)]
-        return parts_x, parts_y
-
     def add_x(home, parts):
         for node, part in zip((0, 7), parts):
             home[node] = home[node] + part
@@ -490,7 +487,8 @@
 
     def add_field(f):
         home = homes[f]
-        parts_x, parts_y = from_sides(f)
+        parts_x = [read_x(ins0.at[f], side) for side in range(2)]
+        parts_y = [read_y(ins0.at[f], side) for side in range(2)]
         add_x(home, parts_x)
         add_y(home, parts_y)
         if f == 0:
@@ -504,25 +502,20 @@
                 first, last = join_x(part[0], part[7])
                 cz[0, node] = cz[0, node] + (first - part[0])
                 cz[7, node] = cz[7, node] + (last - part[7])
-        for k, (ix, iy, _, turn) in enumerate(node_d):
-            home[ix, iy] = home[ix, iy] + jnp.where(halo_d[k], roll_sub(dr0[k, f], turn), 0.0)
-
-    arrive(*group_refs(0))
+        for k, (ix, iy, _) in enumerate(node_d):
+            home[ix, iy] = home[ix, iy] + read_line(ins0.at[f], k)
+
+    receive_group(0)
     add_field(0)
     for c in (0, 7):
         fill_rows(slice(c, c + 1))
 
-    def put_faces(side_x, side_y, fx0, fx1, fy0, fy1):
-        side_x[0], side_x[1] = pack_x(fx0, fx1)
-        side_y[0], side_y[1] = pack_y(fy0, fy1)
-
-    ends = ((xs1, ys1, None), (xrk, yrk, None), sendk, recvk, 0)
-    put_faces(xs1, ys1, kx[0], kx[7], ky[:, 0], ky[:, 7])
-    copies(*ends)
+    put_faces(ends_out, kx[0], kx[7], ky[:, 0], ky[:, 7])
+    post_faces(ends_out, ends_in, send0.at[3], recv0.at[3])
     add_field(1)
 
     def rest_of_setup():
-        arrive(*group_refs(1))
+        receive_group(1)
         for f in groups[1]:
             add_field(f)
         for here in face_parts:
@@ -572,22 +565,13 @@
             along_y = along_y + ky[:, j] * u[:, j]
         return along_x, along_y
 
-    def mail(kind, field, slot):
-        if kind < 2:
-            src = (xs.at[kind, field, slot], ys.at[kind, field, slot], None)
-            dst = (xr.at[kind, field, slot], yr.at[kind, field, slot], None)
-        else:
-            src = (None, None, ds.at[field, slot])
-            dst = (None, None, dr.at[field, slot])
-        return src, dst, send.at[field, slot], recv.at[field, slot], (0, 8, 0)[kind]
-
     def begin(field, turn, source, gradient, v_from, u_to, v_to, between=None):
         slot = lax.rem(turn, 2)
-        first, second = mail(0, field, slot), mail(1, field, slot)
-        corners = mail(2, field, slot)
+        out, into = outs.at[field, slot], ins.at[field, slot]
+        ssem, rsem = send.at[field, slot], recv.at[field, slot]
         own_x, own_y = face_rows(source)
-        put_faces(first[0][0], first[0][1], own_x, own_x, own_y, own_y)
-        copies(*first)
+        put_faces(out.at[0], own_x, own_x, own_y, own_y)
+        post_faces(out.at[0], into.at[0], ssem.at[0], rsem.at[0])
 
         def send_corners():
             for side, node in ((0, 0), (1, 7)):
@@ -595,11 +579,11 @@
                 sp_y[field, side] = scale[:, node] * own_y
             lines_x = [jnp.sum(kx[:, n] * sp_y[field, s], axis=0) for s, n in ((0, 0), (1, 7))]
             lines_y = [jnp.sum(ky[n] * sp_x[field, s], axis=0) for s, n in ((0, 0), (1, 7))]
-            ds[field, slot] = -(
+            lines[field, slot] = -(
                 jnp.where(ey == 0, lines_x[0], lines_x[1])
                 + jnp.where(low_x, lines_y[0], lines_y[1])
             )
-            copies(*corners)
+            post_lines(lines.at[field, slot], into.at[1], ssem.at[2], rsem.at[1])
 
         if between is None:
             send_corners()
@@ -612,8 +596,8 @@
 
             advance(source, gradient, v_from, u_to, v_to, both)
         next_x, next_y = face_rows(u_to)
-        put_faces(second[0][0], second[0][1], next_x, next_x, next_y, next_y)
-        copies(*second)
+        put_faces(out.at[1], next_x, next_x, next_y, next_y)
+        post_faces(out.at[1], into.at[1], ssem.at[1], rsem.at[1])
 
     def mend(u, v, parts_x, parts_y):
         for node, part in zip((0, 7), parts_x):
@@ -626,34 +610,29 @@
             v[:, node] = v[:, node] - part
 
     def complete(field, turn, u, v):
-        letter = mail(0, field, lax.rem(turn, 2))
-        arrive(*letter)
-        from_x, from_y = letter[1][:2]
-        mend(
-            u,
-            v,
-            [jnp.where(halo_x[s], unpack_x(s, from_x[s]), 0.0) for s in range(2)],
-            [jnp.where(halo_y[s], unpack_y(s, from_y[s]), 0.0) for s in range(2)],
-        )
+        slot = lax.rem(turn, 2)
+        out, into = outs.at[field, slot], ins.at[field, slot]
+        sent(out.at[0], send.at[field, slot, 0])
+        sent(out.at[1], send.at[field, slot, 1])
+        sent(out.at[0, pl.ds(0, 4)], send.at[field, slot, 2])
+        received(into.at[0, pl.ds(0, 12)], recv.at[field, slot, 0])
+        parts_x = [read_x(into.at[0], side) for side in range(2)]
+        mend(u, v, parts_x, [read_y(into.at[0], side) for side in range(2)])
 
     def finish(field, turn, source, gradient, v_from, u_to, v_to):
         slot = lax.rem(turn, 2)
+        into = ins.at[field, slot, 1]
         advance(source, gradient, v_from, u_to, v_to)
-        second, corners = mail(1, field, slot), mail(2, field, slot)
-        arrive(*second)
-        from_x, from_y = second[1][:2]
+        received(into, recv.at[field, slot, 1])
         parts_x, parts_y = [], []
         for s in range(2):
-            part = unpack_x(s, from_x[s]) - kn_x[s] * sp_x[field, s]
-            parts_x.append(jnp.where(halo_x[s], part, 0.0))
-            part = unpack_y(s, from_y[s]) - kn_y[s] * sp_y[field, s]
-            parts_y.append(jnp.where(halo_y[s], part, 0.0))
+            part = read_x(into, s) - kn_x[s] * sp_x[field, s]
+            parts_x.append(part)
+            part = read_y(into, s) - kn_y[s] * sp_y[field, s]
+            parts_y.append(part)
         mend(u_to, v_to, parts_x, parts_y)
-        arrive(*corners)
-        from_d = corners[1][2]
-        for k, (ix, iy, _, turn_by) in enumerate(node_d):
-            line = jnp.where(halo_d[k], roll_sub(from_d[k], turn_by), 0.0)
-            part = scale[ix, iy] * line
+        for k, (ix, iy, _) in enumerate(node_d):
+            part = scale[ix, iy] * read_line(into, k)
             u_to[ix, iy] = u_to[ix, iy] - part
             v_to[ix, iy] = v_to[ix, iy] - part
 
@@ -676,16 +655,19 @@
         finish(1, turn, aa.at[n], ga.at[n], va, aa.at[n - 1], va)
 
     begin_u(0, rest_of_setup)
-    arrive(*group_refs(2))
+    receive_group(2)
     for f in groups[2]:
         add_field(f)
     for here in face_parts:
         va[here] = aa[(8, *here)] - va[here]
     begin_a(0)
-    arrive(*ends)
+    received(ends_in, recv0.at[3])
     for side in range(2):
-        kn_x[side] = unpack_x(side, xrk[side])
-        kn_y[side] = unpack_y(side, yrk[side])
+        kn_x[side] = read_x(ends_in, side)
+        kn_y[side] = read_y(ends_in, side)
+    sent(ends_out, send0.at[3])
+    for g, group in enumerate(groups):
+        sent(ins0.at[pl.ds(group[0], len(group))], send0.at[g])
 
     def cycle(turn, carry):
         finish_u(turn)
@@ -747,8 +729,7 @@
             dens_ref[ix, rows, :] = weight * density[iy]
             mod_ref[ix, rows, :] = modulus[iy]
             imp_ref[ix, rows, :] = impedance[iy]
-    arrive(*mail(2, 1, last % 2))
-    arrive(*mail(1, 1, last % 2))
+    received(ins.at[1, last % 2, 1], recv.at[1, last % 2, 1])
 
 
 def deliver(*refs):
@@ -805,29 +786,19 @@
             vectors(2, 8),
             vectors(2, 8),
             field(3),
-            vectors(2, 7, 4),
-            vectors(2, 7, 2),
+            vectors(7, 12),
             vectors(7),
-            vectors(2, 4),
+            vectors(7, 16),
+            vectors(12),
+            vectors(12),
+            vectors(2, 2, 2, 12),
             vectors(2, 2),
-            vectors(2, 7, 4),
-            vectors(2, 7, 2),
-            vectors(4, 7),
-            vectors(2, 4),
-            vectors(2, 2),
-            vectors(2, 2, 2, 2, 4),
-            vectors(2, 2, 2, 2, 2),
-            vectors(2, 2),
-            vectors(2, 2, 2, 2, 4),
-            vectors(2, 2, 2, 2, 2),
-            vectors(2, 2, 4),
+            vectors(2, 2, 2, 16),
             pltpu.SemaphoreType.DMA((13,)),
-            pltpu.SemaphoreType.DMA((24,)),
-            pltpu.SemaphoreType.DMA((24,)),
             pltpu.SemaphoreType.DMA((4,)),
             pltpu.SemaphoreType.DMA((4,)),
-            pltpu.SemaphoreType.DMA((2, 2, 12)),
-            pltpu.SemaphoreType.DMA((2, 2, 12)),
+            pltpu.SemaphoreType.DMA((2, 2, 3)),
+            pltpu.SemaphoreType.DMA((2, 2, 2)),
         ],
         compiler_params=pltpu.CompilerParams(
             collective_id=0, has_side_effects=True, vmem_limit_bytes=48 * 1024 * 1024

time: 31.8 us -> 30.6 us (0.962)
  Pallas kernels: 31.1 us -> 29.9 us
    pallas_call x1, Pallas kernels: 30.1 us -> 28.9 us  [per_device(): pl.pallas_call(functools.partial(kernel, shape_xy), out_shape=(pltpu.VMEM...]
where the time goes in v3:
time: 30.6 us; the launch traced here: 30.5 us
  Pallas kernels  29.9 us (98%)
  between operations  0.64 us (2%)
    pallas_call x1, Pallas kernels, per_device(): pl.pallas_call(functools.partial(kernel, shape_xy), out_shape=(pltpu.VMEM...  28.9 us
    pallas_call x1, Pallas kernels, per_device(): pl.pallas_call(deliver, out_shape=(pltpu.HBM(args[0].shape, F32),) * 3, i...  0.93 us

profile of v3, /device:TPU:7, one launch (start us, length us, event | category | flops | bytes accessed | tf_op | source)
XLA Modules:
  0.0 30.5 jit_solution(6636826905468437178)
XLA Ops:
  0.6 28.9 %shard_map.94 = (f32[8,64,128]{2,1,0:T(8,128)S(1)}, f32[8,64,128]{2,1,0:T(8,128)S(1)}, f32[8,64,128]{2,1,0:T(8,128)S(1)}) custom-call(f32[16,32,128]{2,1,0:T(8,128)} %up_ref.1, f32[16,32,128]{2,1,0:T(8,128)} %uc_ref.1, f32[16,32,128]{2,1,0:T(8,128)} %an_ref.1, f32[16,32,128]{2,1,0:T(8,128)} %ac_ref.1, f32[16,32,128]{2,1,0:T(8,128)} %im_ref.1, ...), custom_call_target="tpu_custom_call" | custom-call | tf_op jit(solution)/shard_map/pallas_call | solution.py:761
  29.6 0.9 %shard_map.95 = (f32[16,32,128]{2,1,0:T(8,128)}, f32[16,32,128]{2,1,0:T(8,128)}, f32[16,32,128]{2,1,0:T(8,128)}) custom-call(f32[8,64,128]{2,1,0:T(8,128)S(1)} %get-tuple-element.6.refs_0_, f32[8,64,128]{2,1,0:T(8,128)S(1)} %get-tuple-element.7.refs_1_, f32[8,64,128]{2,1,0:T(8,128)S(1)} %get-tuple-element.8.refs_2_), custom_call_target="tpu_custom_call" | custom-call | tf_op jit(solution)/shard_map/pallas_call | solution.py:807

commit v4 on v3

--- a/solution.py
+++ b/solution.py
@@ -569,6 +569,13 @@
         slot = lax.rem(turn, 2)
         out, into = outs.at[field, slot], ins.at[field, slot]
         ssem, rsem = send.at[field, slot], recv.at[field, slot]
+
+        def if_needed(post):
+            if field == 0 or isinstance(turn, int):
+                post()
+            else:
+                pl.when(turn < STEPS // 2 - 1)(post)
+
         own_x, own_y = face_rows(source)
         put_faces(out.at[0], own_x, own_x, own_y, own_y)
         post_faces(out.at[0], into.at[0], ssem.at[0], rsem.at[0])
@@ -583,7 +590,10 @@
                 jnp.where(ey == 0, lines_x[0], lines_x[1])
                 + jnp.where(low_x, lines_y[0], lines_y[1])
             )
-            post_lines(lines.at[field, slot], into.at[1], ssem.at[2], rsem.at[1])
+
+            @if_needed
+            def _():
+                post_lines(lines.at[field, slot], into.at[1], ssem.at[2], rsem.at[1])
 
         if between is None:
             send_corners()
@@ -595,9 +605,12 @@
                 send_corners()
 
             advance(source, gradient, v_from, u_to, v_to, both)
-        next_x, next_y = face_rows(u_to)
-        put_faces(out.at[1], next_x, next_x, next_y, next_y)
-        post_faces(out.at[1], into.at[1], ssem.at[1], rsem.at[1])
+
+        @if_needed
+        def _():
+            next_x, next_y = face_rows(u_to)
+            put_faces(out.at[1], next_x, next_x, next_y, next_y)
+            post_faces(out.at[1], into.at[1], ssem.at[1], rsem.at[1])
 
     def mend(u, v, parts_x, parts_y):
         for node, part in zip((0, 7), parts_x):
@@ -609,12 +622,13 @@
             u[:, node] = u[:, node] - part
             v[:, node] = v[:, node] - part
 
-    def complete(field, turn, u, v):
+    def complete(field, turn, u, v, second=True):
         slot = lax.rem(turn, 2)
         out, into = outs.at[field, slot], ins.at[field, slot]
         sent(out.at[0], send.at[field, slot, 0])
-        sent(out.at[1], send.at[field, slot, 1])
-        sent(out.at[0, pl.ds(0, 4)], send.at[field, slot, 2])
+        if second:
+            sent(out.at[1], send.at[field, slot, 1])
+            sent(out.at[0, pl.ds(0, 4)], send.at[field, slot, 2])
         received(into.at[0, pl.ds(0, 12)], recv.at[field, slot, 0])
         parts_x = [read_x(into.at[0], side) for side in range(2)]
         mend(u, v, parts_x, [read_y(into.at[0], side) for side in range(2)])
@@ -706,7 +720,7 @@
         modulus, impedance = moduli_of((7, 8), ix)
         sums[1, ix] = sums[1, ix] + modulus
         sums[2, ix] = sums[2, ix] + impedance
-    complete(1, last, aa.at[1], va)
+    complete(1, last, aa.at[1], va, second=False)
     source, gradient = aa.at[1], ga.at[1]
     gradient[2] = times(source[...].reshape(512, LANES), 0).reshape(8, 8, 8, LANES)
     for c in range(0, 8, CHUNK):
@@ -729,7 +743,6 @@
             dens_ref[ix, rows, :] = weight * density[iy]
             mod_ref[ix, rows, :] = modulus[iy]
             imp_ref[ix, rows, :] = impedance[iy]
-    received(ins.at[1, last % 2, 1], recv.at[1, last % 2, 1])
 
 
 def deliver(*refs):

time: 30.6 us -> 29.9 us (0.977)
  Pallas kernels: 29.9 us -> 29.1 us
    pallas_call x1, Pallas kernels: 28.9 us -> 28.2 us  [per_device(): pl.pallas_call(functools.partial(kernel, shape_xy), out_shape=(pltpu.VMEM...]
where the time goes in v4:
time: 29.9 us; the launch traced here: 29.8 us
  Pallas kernels  29.1 us (97%)
  between operations  0.64 us (2%)
    pallas_call x1, Pallas kernels, per_device(): pl.pallas_call(functools.partial(kernel, shape_xy), out_shape=(pltpu.VMEM...  28.2 us
    pallas_call x1, Pallas kernels, per_device(): pl.pallas_call(deliver, out_shape=(pltpu.HBM(args[0].shape, F32),) * 3, i...  0.93 us

profile of v4, /device:TPU:7, one launch (start us, length us, event | category | flops | bytes accessed | tf_op | source)
XLA Modules:
  0.0 29.8 jit_solution(12576013999059558704)
XLA Ops:
  0.6 28.2 %shard_map.94 = (f32[8,64,128]{2,1,0:T(8,128)S(1)}, f32[8,64,128]{2,1,0:T(8,128)S(1)}, f32[8,64,128]{2,1,0:T(8,128)S(1)}) custom-call(f32[16,32,128]{2,1,0:T(8,128)} %up_ref.1, f32[16,32,128]{2,1,0:T(8,128)} %uc_ref.1, f32[16,32,128]{2,1,0:T(8,128)} %an_ref.1, f32[16,32,128]{2,1,0:T(8,128)} %ac_ref.1, f32[16,32,128]{2,1,0:T(8,128)} %im_ref.1, ...), custom_call_target="tpu_custom_call" | custom-call | tf_op jit(solution)/shard_map/pallas_call | solution.py:774
  28.9 0.9 %shard_map.95 = (f32[16,32,128]{2,1,0:T(8,128)}, f32[16,32,128]{2,1,0:T(8,128)}, f32[16,32,128]{2,1,0:T(8,128)}) custom-call(f32[8,64,128]{2,1,0:T(8,128)S(1)} %get-tuple-element.6.refs_0_, f32[8,64,128]{2,1,0:T(8,128)S(1)} %get-tuple-element.7.refs_1_, f32[8,64,128]{2,1,0:T(8,128)S(1)} %get-tuple-element.8.refs_2_), custom_call_target="tpu_custom_call" | custom-call | tf_op jit(solution)/shard_map/pallas_call | solution.py:820

commit v5 on v4

--- a/solution.py
+++ b/solution.py
@@ -280,8 +280,10 @@
             copy(src, dst, ssem, rsem, device).start()
 
     def post_lines(line, into, ssem, rsem, lead=()):
-        for device, slot in targets_d:
-            copy(line, into.at[(*lead, 12 + slot)], ssem, rsem, device).start()
+        for row, (device, slot) in zip((0, 3, 4, 7), targets_d):
+            src = line.at[(*lead, pl.ds(row, 1))]
+            dst = into.at[(*lead, 12 + slot, pl.ds(row, 1))]
+            copy(src, dst, ssem, rsem, device).start()
 
     def received(into, rsem):
         copy(into, into, rsem, rsem, targets_x[0][0]).wait_recv()
@@ -420,16 +422,20 @@
         here = pl.ds(groups[g][0], len(groups[g]))
         every = (pl.ds(0, len(groups[g])),)
         out, into = outs0.at[here], ins0.at[here]
-        post_lines(lines0.at[here], into, send0.at[g], recv0.at[g], every)
+        post_lines(lines0.at[here], into, send0.at[4 + g], recv0.at[4 + g], every)
         post_faces(out, into, send0.at[g], recv0.at[g], every)
 
     def receive_group(g):
-        received(ins0.at[pl.ds(groups[g][0], len(groups[g]))], recv0.at[g])
+        here = pl.ds(groups[g][0], len(groups[g]))
+        received(ins0.at[here, pl.ds(0, 12)], recv0.at[g])
+        received(lines0.at[here, pl.ds(0, 4)], recv0.at[4 + g])
 
     for f in groups[0]:
         arrived_here(f)
         fill(f, faces_at)
         pack_field(f)
+    pl.semaphore_wait(barrier, 8)
+    post_group(0)
     loads[12].wait()
     faces, third_face = damping_faces()
     for f in groups[1]:
@@ -437,8 +443,6 @@
             arrived_here(f)
         fill(f, faces_at)
         pack_field(f)
-    pl.semaphore_wait(barrier, 8)
-    post_group(0)
     post_group(1)
     for home, joins in ((cz, (join_first, join_second)), (cy, (join_first,)), (cx, (join_second,))):
         for join in joins:
@@ -510,11 +514,11 @@
     for c in (0, 7):
         fill_rows(slice(c, c + 1))
 
-    put_faces(ends_out, kx[0], kx[7], ky[:, 0], ky[:, 7])
-    post_faces(ends_out, ends_in, send0.at[3], recv0.at[3])
     add_field(1)
 
     def rest_of_setup():
+        put_faces(ends_out, kx[0], kx[7], ky[:, 0], ky[:, 7])
+        post_faces(ends_out, ends_in, send0.at[3], recv0.at[3])
         receive_group(1)
         for f in groups[1]:
             add_field(f)
@@ -593,7 +597,7 @@
 
             @if_needed
             def _():
-                post_lines(lines.at[field, slot], into.at[1], ssem.at[2], rsem.at[1])
+                post_lines(lines.at[field, slot], into.at[1], ssem.at[2], rsem.at[2])
 
         if between is None:
             send_corners()
@@ -628,7 +632,7 @@
         sent(out.at[0], send.at[field, slot, 0])
         if second:
             sent(out.at[1], send.at[field, slot, 1])
-            sent(out.at[0, pl.ds(0, 4)], send.at[field, slot, 2])
+            sent(lines.at[field, slot, pl.ds(0, 4)], send.at[field, slot, 2])
         received(into.at[0, pl.ds(0, 12)], recv.at[field, slot, 0])
         parts_x = [read_x(into.at[0], side) for side in range(2)]
         mend(u, v, parts_x, [read_y(into.at[0], side) for side in range(2)])
@@ -637,7 +641,7 @@
         slot = lax.rem(turn, 2)
         into = ins.at[field, slot, 1]
         advance(source, gradient, v_from, u_to, v_to)
-        received(into, recv.at[field, slot, 1])
+        received(into.at[pl.ds(0, 12)], recv.at[field, slot, 1])
         parts_x, parts_y = [], []
         for s in range(2):
             part = read_x(into, s) - kn_x[s] * sp_x[field, s]
@@ -645,6 +649,7 @@
             part = read_y(into, s) - kn_y[s] * sp_y[field, s]
             parts_y.append(part)
         mend(u_to, v_to, parts_x, parts_y)
+        received(lines.at[field, slot, pl.ds(0, 4)], recv.at[field, slot, 2])
         for k, (ix, iy, _) in enumerate(node_d):
             part = scale[ix, iy] * read_line(into, k)
             u_to[ix, iy] = u_to[ix, iy] - part
@@ -681,7 +686,9 @@
         kn_y[side] = read_y(ends_in, side)
     sent(ends_out, send0.at[3])
     for g, group in enumerate(groups):
-        sent(ins0.at[pl.ds(group[0], len(group))], send0.at[g])
+        here = pl.ds(group[0], len(group))
+        sent(outs0.at[here], send0.at[g])
+        sent(lines0.at[here, pl.ds(0, 4)], send0.at[4 + g])
 
     def cycle(turn, carry):
         finish_u(turn)
@@ -808,10 +815,10 @@
             vectors(2, 2),
             vectors(2, 2, 2, 16),
             pltpu.SemaphoreType.DMA((13,)),
-            pltpu.SemaphoreType.DMA((4,)),
-            pltpu.SemaphoreType.DMA((4,)),
+            pltpu.SemaphoreType.DMA((7,)),
+            pltpu.SemaphoreType.DMA((7,)),
             pltpu.SemaphoreType.DMA((2, 2, 3)),
-            pltpu.SemaphoreType.DMA((2, 2, 2)),
+            pltpu.SemaphoreType.DMA((2, 2, 3)),
         ],
         compiler_params=pltpu.CompilerParams(
             collective_id=0, has_side_effects=True, vmem_limit_bytes=48 * 1024 * 1024

time: 29.9 us -> 29.9 us (level)
  no operation moved by 1% of the time
where the time goes in v5:
time: 29.9 us; the launch traced here: 29.8 us
  Pallas kernels  29.1 us (97%)
  between operations  0.64 us (2%)
    pallas_call x1, Pallas kernels, per_device(): pl.pallas_call(functools.partial(kernel, shape_xy), out_shape=(pltpu.VMEM...  28.2 us
    pallas_call x1, Pallas kernels, per_device(): pl.pallas_call(deliver, out_shape=(pltpu.HBM(args[0].shape, F32),) * 3, i...  0.93 us

profile of v5, /device:TPU:7, one launch (start us, length us, event | category | flops | bytes accessed | tf_op | source)
XLA Modules:
  0.0 29.8 jit_solution(12816873279867124517)
XLA Ops:
  0.6 28.2 %shard_map.94 = (f32[8,64,128]{2,1,0:T(8,128)S(1)}, f32[8,64,128]{2,1,0:T(8,128)S(1)}, f32[8,64,128]{2,1,0:T(8,128)S(1)}) custom-call(f32[16,32,128]{2,1,0:T(8,128)} %up_ref.1, f32[16,32,128]{2,1,0:T(8,128)} %uc_ref.1, f32[16,32,128]{2,1,0:T(8,128)} %an_ref.1, f32[16,32,128]{2,1,0:T(8,128)} %ac_ref.1, f32[16,32,128]{2,1,0:T(8,128)} %im_ref.1, ...), custom_call_target="tpu_custom_call" | custom-call | tf_op jit(solution)/shard_map/pallas_call | solution.py:781
  28.8 0.9 %shard_map.95 = (f32[16,32,128]{2,1,0:T(8,128)}, f32[16,32,128]{2,1,0:T(8,128)}, f32[16,32,128]{2,1,0:T(8,128)}) custom-call(f32[8,64,128]{2,1,0:T(8,128)S(1)} %get-tuple-element.6.refs_0_, f32[8,64,128]{2,1,0:T(8,128)S(1)} %get-tuple-element.7.refs_1_, f32[8,64,128]{2,1,0:T(8,128)S(1)} %get-tuple-element.8.refs_2_), custom_call_target="tpu_custom_call" | custom-call | tf_op jit(solution)/shard_map/pallas_call | solution.py:827

commit v6 on v5

--- a/solution.py
+++ b/solution.py
@@ -570,15 +570,13 @@
         return along_x, along_y
 
     def begin(field, turn, source, gradient, v_from, u_to, v_to, between=None):
-        slot = lax.rem(turn, 2)
+        slot = turn % 2
         out, into = outs.at[field, slot], ins.at[field, slot]
         ssem, rsem = send.at[field, slot], recv.at[field, slot]
 
         def if_needed(post):
-            if field == 0 or isinstance(turn, int):
+            if field == 0 or turn < STEPS // 2 - 1:
                 post()
-            else:
-                pl.when(turn < STEPS // 2 - 1)(post)
 
         own_x, own_y = face_rows(source)
         put_faces(out.at[0], own_x, own_x, own_y, own_y)
@@ -627,7 +625,7 @@
             v[:, node] = v[:, node] - part
 
     def complete(field, turn, u, v, second=True):
-        slot = lax.rem(turn, 2)
+        slot = turn % 2
         out, into = outs.at[field, slot], ins.at[field, slot]
         sent(out.at[0], send.at[field, slot, 0])
         if second:
@@ -638,7 +636,7 @@
         mend(u, v, parts_x, [read_y(into.at[0], side) for side in range(2)])
 
     def finish(field, turn, source, gradient, v_from, u_to, v_to):
-        slot = lax.rem(turn, 2)
+        slot = turn % 2
         into = ins.at[field, slot, 1]
         advance(source, gradient, v_from, u_to, v_to)
         received(into.at[pl.ds(0, 12)], recv.at[field, slot, 1])
@@ -697,7 +695,8 @@
         begin_a(turn + 1)
         return carry
 
-    lax.fori_loop(0, STEPS // 2 - 1, cycle, 0)
+    for turn in range(STEPS // 2 - 1):
+        cycle(turn, 0)
 
     def density_of(ns, ix):
         total = None

time: 29.9 us -> 29.6 us (0.990)
  Pallas kernels: 29.1 us -> 28.8 us
    pallas_call x1, Pallas kernels: 28.2 us -> 27.9 us  [per_device(): pl.pallas_call(functools.partial(kernel, shape_xy), out_shape=(pltpu.VMEM...]
where the time goes in v6:
time: 29.6 us; the launch traced here: 29.4 us
  Pallas kernels  28.8 us (97%)
  between operations  0.64 us (2%)
    pallas_call x1, Pallas kernels, per_device(): pl.pallas_call(functools.partial(kernel, shape_xy), out_shape=(pltpu.VMEM...  27.9 us
    pallas_call x1, Pallas kernels, per_device(): pl.pallas_call(deliver, out_shape=(pltpu.HBM(args[0].shape, F32),) * 3, i...  0.93 us

profile of v6, /device:TPU:7, one launch (start us, length us, event | category | flops | bytes accessed | tf_op | source)
XLA Modules:
  0.0 29.4 jit_solution(6250882152016662384)
XLA Ops:
  0.6 27.9 %shard_map.94 = (f32[8,64,128]{2,1,0:T(8,128)S(1)}, f32[8,64,128]{2,1,0:T(8,128)S(1)}, f32[8,64,128]{2,1,0:T(8,128)S(1)}) custom-call(f32[16,32,128]{2,1,0:T(8,128)} %up_ref.1, f32[16,32,128]{2,1,0:T(8,128)} %uc_ref.1, f32[16,32,128]{2,1,0:T(8,128)} %an_ref.1, f32[16,32,128]{2,1,0:T(8,128)} %ac_ref.1, f32[16,32,128]{2,1,0:T(8,128)} %im_ref.1, ...), custom_call_target="tpu_custom_call" | custom-call | tf_op jit(solution)/shard_map/pallas_call | solution.py:780
  28.5 0.9 %shard_map.95 = (f32[16,32,128]{2,1,0:T(8,128)}, f32[16,32,128]{2,1,0:T(8,128)}, f32[16,32,128]{2,1,0:T(8,128)}) custom-call(f32[8,64,128]{2,1,0:T(8,128)S(1)} %get-tuple-element.6.refs_0_, f32[8,64,128]{2,1,0:T(8,128)S(1)} %get-tuple-element.7.refs_1_, f32[8,64,128]{2,1,0:T(8,128)S(1)} %get-tuple-element.8.refs_2_), custom_call_target="tpu_custom_call" | custom-call | tf_op jit(solution)/shard_map/pallas_call | solution.py:826
